TPU v7x, 256 devices: a whole 4x4x8 slice. The times are simulated.
256 devices in a mesh: dp: 16 (over z_hi, y), space: 16 (over z_lo, x, core).
Axes of the slice: x: 4, y: 4, z: 8 (z_hi: 4, z_lo: 2; z = z_hi * 2 + z_lo), core: 2. Of those that a mesh axis runs over, the one named last changes fastest.
Arguments:
- feature_maps: bfloat16 [16, 48, 48, 2048], P('dp', 'space'), may hold values from -12 to 12
- w_atrous: bfloat16 [3, 9, 2048, 256], P(None, None, 'space'), may hold values from -0.046875 to 0.046875
- w_point: bfloat16 [2048, 256], P('space'), may hold values from -0.125 to 0.125
- w_pool: bfloat16 [2048, 256], P('space'), may hold values from -0.125 to 0.125
- bias_branch: float32 [5, 256], P(None, 'space'), may hold values from -4 to 4
- w_proj: bfloat16 [5, 256, 256], P(None, 'space'), may hold values from -0.15625 to 0.15625
- bias_proj: float32 [256], replicated, may hold values from -4 to 4
- cotangent: bfloat16 [16, 48, 48, 256], P('dp', 'space'), may hold values from -6 to 6
Outputs:
- head_out: bfloat16 [16, 48, 48, 256], P('dp', 'space')
- grad_maps: bfloat16 [16, 48, 48, 2048], P('dp', 'space')
- grad_atrous: float32 [3, 9, 2048, 256], P(None, None, 'space')
- grad_point: float32 [2048, 256], P('space')
- grad_pool: float32 [2048, 256], P('space')
- grad_bias: float32 [5, 256], P(None, 'space')
- grad_proj: float32 [5, 256, 256], P(None, 'space')
- grad_proj_bias: float32 [256], replicated
All inputs are finite; a program needn't handle non-finite values.
Results may differ from a plain program's by a relative error of at most 0.029.
Values may be sent and summed in bfloat16 or wider, within the bound.
A program may use at most 192 MiB of HBM per device.

v0:
```python
import jax
import jax.numpy as jnp
from jax import lax
from jax.sharding import PartitionSpec as P

dilations = (6, 12, 18)
margin_cells = 18


def silu_slope(values):
    sigma = jax.nn.sigmoid(values)
    return sigma * (1.0 + values * (1.0 - sigma))


def tap_stack(planes, dilation):
    height = planes.shape[0]
    columns = planes.shape[1]
    padded = jnp.pad(planes, ((margin_cells, margin_cells), (margin_cells, margin_cells), (0, 0)))
    pieces = []
    for row_tap in range(3):
        for col_tap in range(3):
            row_start = margin_cells + (row_tap - 1) * dilation
            col_start = margin_cells + (col_tap - 1) * dilation
            pieces.append(padded[row_start : row_start + height, col_start : col_start + columns])
    return jnp.concatenate(pieces, axis=-1)


def branch_stack(w_atrous, w_point, w_pool):
    in_rows = w_point.shape[0]
    out_cols = w_point.shape[1]
    taps = jnp.transpose(w_atrous.reshape(27, in_rows, out_cols), (1, 0, 2))
    return jnp.concatenate([taps, w_point[:, None], w_pool[:, None]], axis=1)


def body(feature_maps, w_atrous, w_point, w_pool, bias_branch, w_proj, bias_proj, cotangent):
    shards = lax.axis_size("space")
    position = lax.axis_index("space")
    local_map = feature_maps[0]
    rows_here = local_map.shape[0]
    columns = local_map.shape[1]
    channels = local_map.shape[2]
    owned_cols = bias_branch.shape[1]
    branch_cols = w_proj.shape[2]
    height = rows_here * shards
    pixels = height * columns
    row_pixels = rows_here * columns
    weight_stack = branch_stack(w_atrous, w_point, w_pool)
    column_maps = lax.all_to_all(local_map, "space", split_axis=2, concat_axis=0, tiled=True)
    slice_chans = column_maps.shape[2]
    tap_inputs = [
        tap_stack(column_maps, dilation).reshape(pixels, 9 * slice_chans) for dilation in dilations
    ]
    column_flat = column_maps.reshape(pixels, slice_chans)
    pooled_slice = (jnp.sum(column_flat, axis=0, dtype=jnp.float32) / pixels).astype(jnp.bfloat16)
    pool_partial = jnp.dot(pooled_slice[None], w_pool, preferred_element_type=jnp.float32)[0]
    pool_total = lax.psum(pool_partial, "space")
    pool_pre = (
        lax.dynamic_slice_in_dim(pool_total, position * owned_cols, owned_cols) + bias_branch[4]
    )
    by_output = lax.all_to_all(
        weight_stack[:, :28], "space", split_axis=2, concat_axis=0, tiled=True
    )
    tap_weights = by_output.reshape(channels, 28 * owned_cols)
    block_rows = lax.all_gather(local_map, "space", axis=0, tiled=True)
    product = jnp.dot(
        block_rows.reshape(-1, channels), tap_weights, preferred_element_type=jnp.float32
    )
    responses = product.reshape(block_rows.shape[0], columns, 28, owned_cols)
    padded = jnp.pad(
        responses, ((margin_cells, margin_cells), (margin_cells, margin_cells), (0, 0), (0, 0))
    )
    branch_list = []
    for branch_no in range(3):
        dilation = dilations[branch_no]
        summed = jnp.zeros((height, columns, owned_cols), jnp.float32)
        for tap_no in range(9):
            row_start = margin_cells + (tap_no // 3 - 1) * dilation
            col_start = margin_cells + (tap_no % 3 - 1) * dilation
            summed = (
                summed
                + padded[
                    row_start : row_start + height,
                    col_start : col_start + columns,
                    9 * branch_no + tap_no,
                ]
            )
        branch_list.append(summed.reshape(pixels, owned_cols))
    branch_list.append(responses[:, :, 27].reshape(pixels, owned_cols))
    branch_pre = jnp.stack(branch_list, axis=1)
    branch_pre = branch_pre + bias_branch[:4][None]
    activated = jax.nn.silu(branch_pre).astype(jnp.bfloat16)
    pool_act = jax.nn.silu(pool_pre).astype(jnp.bfloat16)
    joined_local = jnp.concatenate(
        [activated, jnp.broadcast_to(pool_act[None, None], (pixels, 1, owned_cols))], axis=1
    )
    joined_flat = joined_local.reshape(pixels, 5 * owned_cols)
    proj_flat = w_proj.reshape(5 * owned_cols, branch_cols)
    head_sum = lax.psum_scatter(
        jnp.dot(joined_flat, proj_flat, preferred_element_type=jnp.float32).astype(jnp.bfloat16),
        "space",
        scatter_dimension=0,
        tiled=True,
    ).astype(jnp.float32)
    head_pre = head_sum + bias_proj
    head_out = (
        jax.nn.silu(head_pre).astype(jnp.bfloat16).reshape(1, rows_here, columns, branch_cols)
    )
    grad_out = (
        cotangent[0].reshape(row_pixels, branch_cols).astype(jnp.float32) * silu_slope(head_pre)
    ).astype(jnp.bfloat16)
    grad_whole = lax.all_gather(grad_out, "space", axis=0, tiled=True)
    grad_act = jnp.dot(grad_whole, proj_flat.T, preferred_element_type=jnp.float32).reshape(
        pixels, 5, owned_cols
    )
    grad_proj = jnp.dot(joined_flat.T, grad_whole, preferred_element_type=jnp.float32).reshape(
        5, owned_cols, branch_cols
    )
    grad_proj_bias = jnp.sum(grad_whole, axis=0, dtype=jnp.float32)
    grad_pre = (grad_act[:, :4] * silu_slope(branch_pre)).astype(jnp.bfloat16)
    grad_pool_pre = (silu_slope(pool_pre) * jnp.sum(grad_act[:, 4], axis=0)).astype(jnp.bfloat16)
    pool_term = grad_pool_pre.astype(jnp.float32)
    grad_bias = jnp.concatenate(
        [jnp.sum(grad_pre, axis=0, dtype=jnp.float32), pool_term[None]], axis=0
    )
    grad_all, pool_all = (
        lax.all_gather(grad_pre, "space", axis=2, tiled=True),
        lax.all_gather(grad_pool_pre.reshape(1, 1, owned_cols), "space", axis=2, tiled=True),
    )
    pool_full = pool_all.reshape(branch_cols).astype(jnp.float32)
    grad_pool = pooled_slice.astype(jnp.float32)[:, None] * pool_full[None]
    pool_back = (
        jnp.dot(weight_stack[:, 28].astype(jnp.float32), pool_full, precision=lax.Precision.HIGHEST)
        / pixels
    )
    grad_input = (
        jnp.dot(grad_all[:, 3], weight_stack[:, 27].T, preferred_element_type=jnp.float32)
        + pool_back[None]
    )
    grad_cols = []
    for branch_no in range(3):
        dilation = dilations[branch_no]
        branch_grad = grad_all[:, branch_no]
        padded_grad = jnp.pad(
            branch_grad.reshape(height, columns, branch_cols),
            ((margin_cells, margin_cells), (margin_cells, margin_cells), (0, 0)),
        )
        for row_tap in range(3):
            row_start = margin_cells - (row_tap - 1) * dilation
            pieces = []
            for col_tap in range(3):
                col_start = margin_cells - (col_tap - 1) * dilation
                pieces.append(
                    padded_grad[row_start : row_start + height, col_start : col_start + columns]
                )
            spread = jnp.concatenate(pieces, axis=-1).reshape(pixels, 3 * branch_cols)
            first_tap = 9 * branch_no + 3 * row_tap
            weights = jnp.transpose(weight_stack[:, first_tap : first_tap + 3], (1, 2, 0)).reshape(
                3 * branch_cols, slice_chans
            )
            grad_input = grad_input + jnp.dot(spread, weights, preferred_element_type=jnp.float32)
        tap_grad = jnp.dot(tap_inputs[branch_no].T, branch_grad, preferred_element_type=jnp.float32)
        grad_cols.append(jnp.transpose(tap_grad.reshape(9, slice_chans, branch_cols), (1, 0, 2)))
    point_grad = jnp.dot(column_flat.T, grad_all[:, 3], preferred_element_type=jnp.float32)
    grad_cols.append(point_grad[:, None])
    kernel_grads = jnp.concatenate(grad_cols, axis=1)
    kernel_grads, grad_pool, grad_bias, grad_proj, grad_proj_bias = (
        lax.psum(kernel_grads.astype(jnp.bfloat16), "dp").astype(jnp.float32),
        lax.psum(grad_pool.astype(jnp.bfloat16), "dp").astype(jnp.float32),
        lax.psum(grad_bias.astype(jnp.bfloat16), "dp").astype(jnp.float32),
        lax.psum(grad_proj.astype(jnp.bfloat16), "dp").astype(jnp.float32),
        lax.psum(grad_proj_bias.astype(jnp.bfloat16), "dp").astype(jnp.float32),
    )
    grad_atrous = jnp.transpose(
        kernel_grads[:, :27].reshape(slice_chans, 3, 9, branch_cols), (1, 2, 0, 3)
    )
    grad_point = kernel_grads[:, 27]
    input_local = grad_input.astype(jnp.bfloat16).reshape(height, columns, slice_chans)
    grad_maps = lax.all_to_all(
        input_local, "space", split_axis=0, concat_axis=2, tiled=True
    ).reshape(1, rows_here, columns, channels)
    return (
        head_out,
        grad_maps,
        grad_atrous,
        grad_point,
        grad_pool,
        grad_bias,
        grad_proj,
        grad_proj_bias,
    )


def solution(mesh):
    placed = (
        P("dp", "space", None, None),
        P(None, None, "space", None),
        P("space", None),
        P("space", None),
        P(None, "space"),
        P(None, "space", None),
        P(),
        P("dp", "space", None, None),
    )
    return jax.shard_map(
        body,
        mesh=mesh,
        in_specs=placed,
        out_specs=(
            P("dp", "space", None, None),
            P("dp", "space", None, None),
            P(None, None, "space", None),
            P("space", None),
            P("space", None),
            P(None, "space"),
            P(None, "space", None),
            P(),
        ),
        check_vma=False,
    )
```

profile of v0, /device:TPU:32, one launch (start us, length us, event | category | flops | bytes accessed | tf_op | source)
XLA Modules:
  0.0 571.0 jit_solution(1634832553844885694)
XLA Ops:
  7.9 4.0 copy.70
  11.9 2.0 bitcast_bitcast_fusion
  13.9 3.1 reshape.510
  17.1 5.8 %all-to-all-start.1 = ((bf16[16,2,9216]{2,1,0:T(2,128)(2,1)}), bf16[16,2,9216]{2,1,0:T(2,128)(2,1)S(1)}, u32[]{:S(2)}, u32[]{:S(2)}) async-start(bf16[16,2,9216]{2,1,0:T(2,128)(2,1)} %reshape.510), calls=%async_computation.1 | async-start | bytes 1179648 | tf_op jit(solution)/shard_map/all_to_all | solution.py:48
  23.0 2.8 copy.64
  25.9 2.5 copy.66
  28.5 10.9 %all-to-all-done.1 = bf16[16,2,9216]{2,1,0:T(2,128)(2,1)S(1)} async-done(((bf16[16,2,9216]{2,1,0:T(2,128)(2,1)}), bf16[16,2,9216]{2,1,0:T(2,128)(2,1)S(1)}, u32[]{:S(2)}, u32[]{:S(2)}) %all-to-all-start.1) | async-done | bytes 589856 | tf_op jit(solution)/shard_map/all_to_all | solution.py:48
  39.3 5.6 all-to-all-start
  45.1 2.8 reshape.511
  49.4 61.7 %psum.42 = f32[256]{0:T(256)S(1)} all-reduce(f32[256]{0:T(256)S(1)} %bitcast.298), channel_id=1, replica_groups=mesh['dp'=16,'space'=16] {'space'}, use_global_device_ids=true, to_apply=%region_1.2 | all-reduce | flops 256 | bytes 2048 | tf_op jit(solution)/shard_map/psum | solution.py:56
  111.2 4.0 copy.68
  115.2 10.6 %convolution_bitcast_fusion = f32[2304,448]{0,1:T(8,128)} fusion(bf16[2304,2048]{1,0:T(8,128)(2,1)} %bitcast.300, bf16[56,8,16,128]{3,2,1,0:T(8,128)(2,1)} %bitcast.286), kind=kOutput, calls=%fused_computation.72 | convolution fusion | flops 4227858432 | bytes 15400960 | tf_op jit(solution)/shard_map/dot_general | solution.py:65
  125.9 10.7 %reshape.456 = f32[48,48,28,16]{1,0,3,2:T(8,128)} reshape(f32[2304,448]{0,1:T(8,128)} %convolution_bitcast_fusion) | data formatting | bytes 8257536 | tf_op jit(solution)/shard_map/reshape | solution.py:68
  136.6 6.3 %fusion.41 = (f32[48,48,1,16]{1,0,3,2:T(8,128)}, f32[48,48,1,16]{1,0,3,2:T(8,128)S(1)}, f32[48,48,1,16]{1,0,3,2:T(8,128)S(1)}, f32[48,48,1,16]{1,0,3,2:T(8,128)S(1)}) fusion(f32[48,48,28,16]{1,0,3,2:T(8,128)} %reshape.456), kind=kLoop, calls=%fused_computation.143 | loop fusion | flops 884736 | bytes 13172736 | tf_op jit(solution)/shard_map/add | solution.py:80
  148.8 63.2 %reduce-scatter.2.cloned.1.call-done = bf16[144,256]{1,0:T(8,128)(2,1)} async-done(((bf16[2304,256]{1,0:T(8,128)(2,1)}), bf16[144,256]{1,0:T(8,128)(2,1)}) %reduce-scatter.2.cloned.1.call-update) | async-done | bytes 73744 | tf_op jit(solution)/shard_map/reduce_scatter | solution.py:98
  215.2 2.8 fusion.77
  218.9 1.7 pad_slice_fusion.47
  221.6 12.4 %pad_slice_fusion.40 = (bf16[48,48,128]{2,1,0:T(8,128)(2,1)}, bf16[48,48,128]{2,1,0:T(8,128)(2,1)}, bf16[48,48,128]{2,1,0:T(8,128)(2,1)}, bf16[48,48,128]{2,1,0:...) fusion(bf16[48,48,128]{2,1,0:T(8,128)(2,1)S(1)} %bitcast.238), kind=kLoop, calls=%fused_computation.40 | loop fusion | bytes 11796480 | tf_op jit(solution)/shard_map/slice | solution.py:24
  234.8 13.8 %all-gather.6.cloned.1.call-done = bf16[2304,256]{1,0:T(8,128)(2,1)} async-done(((bf16[144,256]{1,0:T(8,128)(2,1)}), bf16[2304,256]{1,0:T(8,128)(2,1)}) %all-gather.6.cloned.1.call-update) | async-done | bytes 1179664 | tf_op jit(solution)/shard_map/all_gather | solution.py:111
  248.6 1.8 fusion.27
  250.4 2.0 fusion.75
  252.5 2.1 constant_dynamic-update-slice_fusion.26
  254.7 2.1 constant_dynamic-update-slice_fusion.7
  256.8 2.0 constant_dynamic-update-slice_fusion.6
  270.6 8.6 %copy.84 = bf16[1152,2304]{1,0:T(8,128)(2,1)} copy(bf16[1152,2304]{0,1:T(8,128)(2,1)} %bitcast.74) | data formatting | bytes 10616832 | tf_op jit(solution)/shard_map/dot_general | solution.py:161
  281.9 8.7 %copy.86 = bf16[1152,2304]{1,0:T(8,128)(2,1)} copy(bf16[1152,2304]{0,1:T(8,128)(2,1)} %bitcast.241) | data formatting | bytes 10616832 | tf_op jit(solution)/shard_map/dot_general | solution.py:161
  294.2 8.5 %copy.88 = bf16[1152,2304]{1,0:T(8,128)(2,1)} copy(bf16[1152,2304]{0,1:T(8,128)(2,1)} %bitcast.99) | data formatting | bytes 10616832 | tf_op jit(solution)/shard_map/dot_general | solution.py:161
  303.2 29.4 %all-reduce.5 = bf16[256]{0:T(256)(128)(2,1)S(1)} all-reduce(bf16[256]{0:T(256)(128)(2,1)S(1)} %dynamic-update-slice), channel_id=3, replica_groups=mesh['dp'=16,'space'=16] {'space'}, use_global_device_ids=true, to_apply=%add.5 | all-reduce | flops 256 | bytes 1024
  333.5 4.3 slice_bitcast_fusion.4
  342.2 7.6 %pad_slice_fusion.66 = (bf16[48,48,256]{2,1,0:T(8,128)(2,1)}, bf16[48,48,256]{2,1,0:T(8,128)(2,1)}, bf16[48,48,256]{2,1,0:T(8,128)(2,1)}, bf16[48,48,256]{2,1,0:...) fusion(bf16[48,48,256]{2,1,0:T(8,128)(2,1)} %bitcast.255), kind=kLoop, calls=%fused_computation.66 | loop fusion | bytes 10616832 | tf_op jit(solution)/shard_map/slice | solution.py:153
  349.8 2.4 copy.73
  353.8 3.8 pad_slice_fusion.58
  357.5 2.4 copy.76
  361.4 5.9 %pad_slice_fusion.50 = (bf16[48,48,256]{2,1,0:T(8,128)(2,1)S(1)}, bf16[48,48,256]{2,1,0:T(8,128)(2,1)S(1)}, bf16[48,48,256]{2,1,0:T(8,128)(2,1)}, bf16[48,48,256...) fusion(bf16[48,48,256]{2,1,0:T(8,128)(2,1)} %bitcast.251), kind=kLoop, calls=%fused_computation.50 | loop fusion | bytes 10616832 | tf_op jit(solution)/shard_map/slice | solution.py:153
  367.4 2.0 fusion.29
  369.4 4.6 fusion.19
  374.0 3.0 fusion.20
  377.0 2.9 fusion.21
  381.4 2.2 pad_maximum_fusion.1
  385.3 1.8 convolution_add_fusion.9
  400.3 2.0 pad_maximum_fusion.4
  402.4 2.1 convolution_add_fusion.2
  406.8 3.3 convolution_add_fusion.1
  410.1 1.9 fusion.1
  412.0 4.3 all-to-all-start.2
  417.0 88.1 %all-reduce.6 = (bf16[5,16]{1,0:T(8,128)(2,1)S(1)}, bf16[5,16,256]{2,1,0:T(8,128)(2,1)S(1)}, bf16[256]{0:T(256)(128)(2,1)S(1)}) all-reduce(bf16[5,16]{1,0:T(8,128)(2,1)S(1)} %pad_maximum_fusion.11, bf16[5,16,256]{2,1,0:T(8,128)(2,1)S(1)} %fusion.30, bf16[256]{0:T(256)(128)(2,1)S(1)} %reduce_sum.42), channel_id=1, replica_groups=mesh['dp'=16,'space'=16] {'dp'}, use_global_device_ids=true, to_apply=%region_7.8 | all-reduce | flops 20816 | bytes 83264 | tf_op jit(solution)/shard_map/psum | solution.py:169
  508.2 50.1 %all-reduce.10.cloned.1.call-done = (bf16[128,28,256]{2,0,1:T(8,128)(2,1)}, bf16[128,256]{1,0:T(8,128)(2,1)}) async-done(((bf16[128,28,256]{2,0,1:T(8,128)(2,1)}, bf16[128,256]{1,0:T(8,128)(2,1)}), (bf16[128,28,256]{2,0,1:T(8,128)(2,1)}, bf16[128,256]{1,0:T(8,128)(2,1)})) %all-reduce.10.cloned.1.call-update) | async-done | bytes 1900560 | tf_op jit(solution)/shard_map/psum | solution.py:167
  558.3 3.8 slice.409
  (232 shorter events, 65.1 us)
Async XLA Ops:
  7.2 42.1 %copy-start = (bf16[128,256]{1,0:T(8,128)(2,1)S(1)}, bf16[128,256]{1,0:T(8,128)(2,1)}, u32[]{:S(2)}) copy-start(bf16[128,256]{1,0:T(8,128)(2,1)} %param.11) | copy-start | bytes 196612
  7.2 108.0 %all-gather.10.cloned.1.call-start = ((), (), s32[]{:S(2)}) async-start(), calls=%async_computation.7 | async-start | bytes 10027008 | tf_op jit(solution)/shard_map/all_gather | solution.py:64
  11.9 10.9 %copy-start.56 = (bf16[128,256]{1,0:T(8,128)(2,1)S(1)}, bf16[128,256]{1,0:T(8,128)(2,1)}, u32[]{:S(2)}) copy-start(bf16[128,256]{1,0:T(8,128)(2,1)} %param.10) | copy-start | bytes 196612
  17.1 22.3 %all-to-all-start.1 = ((bf16[16,2,9216]{2,1,0:T(2,128)(2,1)}), bf16[16,2,9216]{2,1,0:T(2,128)(2,1)S(1)}, u32[]{:S(2)}, u32[]{:S(2)}) async-start(bf16[16,2,9216]{2,1,0:T(2,128)(2,1)} %reshape.510), calls=%async_computation.1 | async-start | bytes 1179648 | tf_op jit(solution)/shard_map/all_to_all | solution.py:48
  25.9 19.1 %copy-start.64 = (f32[5,16]{1,0:T(8,128)S(1)}, f32[5,16]{1,0:T(8,128)}, u32[]{:S(2)}) copy-start(f32[5,16]{1,0:T(8,128)} %param.12) | copy-start | bytes 964
  39.3 71.9 %all-to-all-start = ((bf16[128,28,256]{0,1,2:T(8,128)(2,1)}), bf16[128,28,256]{0,1,2:T(8,128)(2,1)}, u32[]{:S(2)}, u32[]{:S(2)}) async-start(bf16[128,28,256]{0,1,2:T(8,128)(2,1)} %copy.66), calls=%async_computation | async-start | bytes 4194304 | tf_op jit(solution)/shard_map/all_to_all | solution.py:60
  45.0 167.0 %reduce-scatter.2.cloned.1.call-start = ((), (), s32[]{:S(2)}) async-start(), calls=%async_computation.4 | async-start | bytes 1253376 | tf_op jit(solution)/shard_map/reduce_scatter | solution.py:98
  136.6 10.6 %copy-start.63 = (bf16[5,16,256]{2,1,0:T(8,128)(2,1)S(1)}, bf16[5,16,256]{2,1,0:T(8,128)(2,1)}, u32[]{:S(2)}) copy-start(bf16[5,16,256]{2,1,0:T(8,128)(2,1)} %param.13) | copy-start | bytes 122884
  144.0 4.7 copy-start.37
  145.1 3.7 copy-start.40
  145.1 66.9 %copy-start.61 = (bf16[1,3,48,256]{3,2,1,0:T(8,128)(2,1)S(1)}, bf16[1,3,48,256]{3,2,1,0:T(8,128)(2,1)}, u32[]{:S(2)}) copy-start(bf16[1,3,48,256]{3,2,1,0:T(8,128)(2,1)} %param.15) | copy-start | bytes 221188
  145.1 66.9 %copy-start.65 = (f32[256]{0:T(256)S(1)}, f32[256]{0:T(256)}, u32[]{:S(2)}) copy-start(f32[256]{0:T(256)} %param.14) | copy-start | bytes 3076
  145.3 72.7 %copy-start.41 = (f32[2304,1,16]{0,2,1:T(8,128)}, f32[2304,1,16]{0,2,1:T(8,128)S(1)}, u32[]{:S(2)}) copy-start(f32[2304,1,16]{0,2,1:T(8,128)S(1)} %stack_reshape_squeeze.3) | copy-start | bytes 442372
  145.3 68.6 %copy-start.66 = (u32[256]{0:T(256)S(1)}, u32[256]{0:T(256)}, u32[]{:S(2)}) copy-start(u32[256]{0:T(256)} %constant.45) | copy-start | bytes 3076
  148.8 99.8 %all-gather.6.cloned.1.call-start = ((), (), s32[]{:S(2)}) async-start(), calls=%async_computation.5 | async-start | bytes 1253376 | tf_op jit(solution)/shard_map/all_gather | solution.py:111
  213.7 119.8 %all-gather.8.cloned.1.call-start = ((), (), s32[]{:S(2)}) async-start(), calls=%async_computation.6 | async-start | bytes 5013504 | tf_op jit(solution)/shard_map/all_gather | solution.py:126
  221.6 28.8 %copy-start.38 = (f32[2304,1,16]{0,2,1:T(8,128)S(1)}, f32[2304,1,16]{0,2,1:T(8,128)}, u32[]{:S(2)}) copy-start(f32[2304,1,16]{0,2,1:T(8,128)} %copy-done.37) | copy-start | bytes 442372
  221.6 28.9 %copy-start.39 = (f32[2304,1,16]{0,2,1:T(8,128)S(1)}, f32[2304,1,16]{0,2,1:T(8,128)}, u32[]{:S(2)}) copy-start(f32[2304,1,16]{0,2,1:T(8,128)} %reshape.490) | copy-start | bytes 442372
  252.4 305.8 %all-reduce.10.cloned.1.call-start = ((), (), s32[]{:S(2)}) async-start(), calls=%async_computation.8 | async-start | bytes 3801088 | tf_op jit(solution)/shard_map/psum | solution.py:167
  252.5 6.3 %copy-start.30 = (bf16[48,48,128]{2,1,0:T(8,128)(2,1)S(1)}, bf16[48,48,128]{2,1,0:T(8,128)(2,1)}, u32[]{:S(2)}) copy-start(bf16[48,48,128]{2,1,0:T(8,128)(2,1)} %get-tuple-element.64) | copy-start | bytes 1769476
  252.5 7.2 %copy-start.29 = (bf16[48,48,128]{2,1,0:T(8,128)(2,1)S(1)}, bf16[48,48,128]{2,1,0:T(8,128)(2,1)}, u32[]{:S(2)}) copy-start(bf16[48,48,128]{2,1,0:T(8,128)(2,1)} %get-tuple-element.69) | copy-start | bytes 1769476
  252.5 8.1 %copy-start.28 = (bf16[48,48,128]{2,1,0:T(8,128)(2,1)S(1)}, bf16[48,48,128]{2,1,0:T(8,128)(2,1)}, u32[]{:S(2)}) copy-start(bf16[48,48,128]{2,1,0:T(8,128)(2,1)} %get-tuple-element.70) | copy-start | bytes 1769476
  252.5 9.0 %copy-start.27 = (bf16[48,48,128]{2,1,0:T(8,128)(2,1)S(1)}, bf16[48,48,128]{2,1,0:T(8,128)(2,1)}, u32[]{:S(2)}) copy-start(bf16[48,48,128]{2,1,0:T(8,128)(2,1)} %get-tuple-element.71) | copy-start | bytes 1769476
  254.7 7.8 %copy-start.26 = (bf16[48,48,128]{2,1,0:T(8,128)(2,1)S(1)}, bf16[48,48,128]{2,1,0:T(8,128)(2,1)}, u32[]{:S(2)}) copy-start(bf16[48,48,128]{2,1,0:T(8,128)(2,1)} %get-tuple-element.77) | copy-start | bytes 1769476
  256.8 6.6 %copy-start.25 = (bf16[48,48,128]{2,1,0:T(8,128)(2,1)S(1)}, bf16[48,48,128]{2,1,0:T(8,128)(2,1)}, u32[]{:S(2)}) copy-start(bf16[48,48,128]{2,1,0:T(8,128)(2,1)} %get-tuple-element.78) | copy-start | bytes 1769476
  258.8 5.5 copy-start.24
  261.6 5.1 copy-start.31
  261.6 5.1 copy-start.32
  263.4 4.4 copy-start.23
  264.3 4.3 copy-start.22
  265.2 4.4 copy-start.21
  281.9 8.7 %copy-start.36 = (bf16[48,48,128]{2,1,0:T(8,128)(2,1)S(1)}, bf16[48,48,128]{2,1,0:T(8,128)(2,1)}, u32[]{:S(2)}) copy-start(bf16[48,48,128]{2,1,0:T(8,128)(2,1)} %get-tuple-element.84) | copy-start | bytes 1769476
  281.9 9.6 %copy-start.35 = (bf16[48,48,128]{2,1,0:T(8,128)(2,1)S(1)}, bf16[48,48,128]{2,1,0:T(8,128)(2,1)}, u32[]{:S(2)}) copy-start(bf16[48,48,128]{2,1,0:T(8,128)(2,1)} %get-tuple-element.85) | copy-start | bytes 1769476
  281.9 10.5 %copy-start.34 = (bf16[48,48,128]{2,1,0:T(8,128)(2,1)S(1)}, bf16[48,48,128]{2,1,0:T(8,128)(2,1)}, u32[]{:S(2)}) copy-start(bf16[48,48,128]{2,1,0:T(8,128)(2,1)} %get-tuple-element.86) | copy-start | bytes 1769476
  367.4 6.6 %slice-start = ((s8[5308416]{0:T(1024)(128)(4,1)}), s8[4194304]{0:T(1024)(128)(4,1)S(1)}, s32[]{:S(2)}) async-start(s8[5308416]{0:T(1024)(128)(4,1)} %bitcast.243), calls=%async_computation.9 | async-start | bytes 8388608
  369.4 4.6 slice-start.1
  369.4 7.6 %slice-start.2 = ((s8[5308416]{0:T(1024)(128)(4,1)}), s8[4194304]{0:T(1024)(128)(4,1)S(1)}, s32[]{:S(2)}) async-start(s8[5308416]{0:T(1024)(128)(4,1)} %bitcast.246), calls=%async_computation.11 | async-start | bytes 8388608
  374.0 3.0 slice-start.3
  381.4 3.0 copy-start.18
  390.5 3.1 copy-start.15
  402.4 3.7 copy-start.19
  406.8 3.3 copy-start.2
  406.8 3.3 copy-start.50
  410.1 6.2 %copy-start.5 = (bf16[2304,256]{1,0:T(8,128)(2,1)S(1)}, bf16[2304,256]{1,0:T(8,128)(2,1)}, u32[]{:S(2)}) copy-start(bf16[2304,256]{1,0:T(8,128)(2,1)} %all-gather.6.cloned.1.call-done) | copy-start | bytes 3538948
  410.1 6.6 %copy-start.47 = (bf16[2304,4,16]{0,2,1:T(8,128)(2,1)S(1)}, bf16[2304,4,16]{0,2,1:T(8,128)(2,1)}, u32[]{:S(2)}) copy-start(bf16[2304,4,16]{0,2,1:T(8,128)(2,1)} %copy-done.46) | copy-start | bytes 884740
  412.0 94.9 %all-to-all-start.2 = ((bf16[48,48,128]{2,1,0:T(8,128)(2,1)}), bf16[48,48,128]{2,1,0:T(8,128)(2,1)S(1)}, u32[]{:S(2)}, u32[]{:S(2)}) async-start(bf16[48,48,128]{2,1,0:T(8,128)(2,1)} %bitcast.59), calls=%async_computation.3 | async-start | bytes 1179648 | tf_op jit(solution)/shard_map/all_to_all | solution.py:178
  558.2 3.9 copy-start.4
  558.2 6.0 %copy-start.1 = (bf16[128,256]{1,0:T(8,128)(2,1)S(1)}, bf16[128,256]{1,0:T(8,128)(2,1)}, u32[]{:S(2)}) copy-start(bf16[128,256]{1,0:T(8,128)(2,1)} %param.11) | copy-start | bytes 196612
  (31 other events, 56.7 us)
Sparse Core Ops, SparseCore 0:
  9.9 90.5 all-gather.9
  148.9 63.0 reduce-scatter.1
  214.4 34.1 all-gather.5
  252.6 40.8 all-gather.7
  381.5 176.6 all-reduce.9
where the time goes:
time: 579 us; the launch traced here: 571 us
  blocking collectives  179 us (31%)
  local copies, waits for them, and re-layouts  156 us (27%)
  waiting for transfers between devices  139 us (24%)
  matrix products  43.2 us (7%)
  other arithmetic  22.5 us (4%)
  starting transfers between devices  16.1 us (3%)
  between operations  15.4 us (3%)
    psum x1, blocking collectives, body(): lax.psum(grad_bias.astype(jnp.bfloat16), 'dp').astype(jnp.float32)  88.1 us
    reduce_scatter x1, waiting for transfers between devices, body(): lax.psum_scatter(jnp.dot(joined_flat, proj_flat, preferred_element_type=j...  63.2 us
    psum x1, blocking collectives, body(): pool_total = lax.psum(pool_partial, 'space')  61.7 us
    psum x1, waiting for transfers between devices, body(): lax.psum(kernel_grads.astype(jnp.bfloat16), 'dp').astype(jnp.float32)  50.1 us
    unnamed x173, local copies, waits for them, and re-layouts  46.8 us
    unnamed x1, blocking collectives  29.4 us
    dot_general x3, local copies, waits for them, and re-layouts, body(): jnp.dot(tap_inputs[branch_no].T, branch_grad, preferred_element_type=jnp....  25.8 us
    slice x3, local copies, waits for them, and re-layouts, body(): padded_grad[row_start:row_start + height, col_start:col_start + columns]  17.3 us
  transfers between devices with their start and end apart: 8, of which 4 were waited for; matrix products, arithmetic and copies ran while one was open for 21% of the time, Pallas kernels for 0%

commit v1 on v0

v1 whole, which is shorter than its diff:
```python
import jax
import jax.numpy as jnp
from jax import lax
from jax.experimental import pallas as pl
from jax.experimental.pallas import tpu as pltpu
from jax.sharding import PartitionSpec as P

bf16 = jnp.bfloat16
f32 = jnp.float32
dilations = (6, 12, 18)
MESH = pl.DeviceIdType.MESH
ROWS = 144
PIX = 2304
PAD = 864
NT = (((1,), (1,)), ((), ()))
TN = (((0,), (0,)), ((), ()))
BLOCK = 576
VMEM_LIMIT = 60 * 2**20


def silu_slope(values):
    sigma = jax.nn.sigmoid(values)
    return sigma * (1.0 + values * (1.0 - sigma))


def dot(a, b):
    return jnp.dot(a, b, preferred_element_type=f32)


def dot_nt(a, b):
    return lax.dot_general(a, b, NT, preferred_element_type=f32)


def aligned(value, step=16):
    return value if isinstance(value, int) else pl.multiple_of(value, step)


class Links:
    def __init__(self, dp, space):
        self.dp = dp
        self.space = space
        self.sent = []

    def copy(self, src, dst, ssem, rsem, dp, space):
        return pltpu.make_async_remote_copy(
            src_ref=src, dst_ref=dst, send_sem=ssem, recv_sem=rsem, device_id=(dp, space), device_id_type=MESH
        )

    def send(self, src, dst, ssem, rsem, dp=None, space=None):
        c = self.copy(src, dst, ssem, rsem, self.dp if dp is None else dp, self.space if space is None else space)
        c.start()
        self.sent.append(c)

    def arrived(self, ref, rsem):
        self.copy(ref, ref, rsem, rsem, self.dp, self.space).wait_recv()

    def flush(self):
        for c in self.sent:
            c.wait_send()


def shifted(block, d, rows, sign):
    lanes = block.shape[1]
    v = block.reshape(rows, 48, lanes)
    col = lax.broadcasted_iota(jnp.int32, (rows, 48, lanes), 1)
    if sign < 0:
        v = jnp.where(col >= d, pltpu.roll(v, d, 1), 0.0)
    else:
        v = jnp.where(col < 48 - d, pltpu.roll(v, 48 - d, 1), 0.0)
    return v.reshape(rows * 48, lanes)


def forward_kernel(
    maps, w, w_point, w_pool, small, w_proj, bias_proj, cot,
    head_out, grad_pre, x_out, g_proj, sums, pool_out, pooled_out,
    x, c, part, core_out, core_in, acc, sa, sb, ra, rb, s2p, s2m, r2p, r2m, sz, rz, wp, msg, msgs,
    x_s, x_r, wp_s, wp_r, msg_s, msg_r, rs_s, rs_r,
):
    dp = lax.axis_index("dp")
    s = lax.axis_index("space")
    core = s % 2
    cx = (s // 2) % 4
    cz = s // 8
    xp = (cx + 1) % 4
    xm = (cx + 3) % 4
    x2 = (cx + 2) % 4
    right = (cz * 4 + xp) * 2 + core
    left = (cz * 4 + xm) * 2 + core
    other_z = ((1 - cz) * 4 + cx) * 2 + core
    sibling = (cz * 4 + cx) * 2 + 1 - core
    links = Links(dp, s)

    barrier = pltpu.get_barrier_semaphore()

    @pl.loop(1, 16)
    def _(o):
        pl.semaphore_signal(barrier, inc=1, device_id=(dp, (s + o) % 16), device_id_type=MESH)

    pl.semaphore_wait(barrier, 15)

    def map_copy(o):
        t = (s + o) % 16
        return links.copy(
            maps.at[:, pl.ds(aligned(t * 128, 128), 128)], x.at[pl.ds(aligned(s * ROWS), ROWS)],
            x_s.at[o], x_r.at[o], dp, t,
        )

    def proj_copy(o):
        part_rows = wp.at[:, pl.ds(aligned(s * 16), 16)]
        return links.copy(w_proj, part_rows, wp_s.at[o], wp_r.at[o], dp, (s + o) % 16)

    def msg_copy(o):
        return links.copy(msg, msgs.at[s], msg_s.at[o], msg_r.at[o], dp, (s + o) % 16)

    @pl.loop(1, 16)
    def _(o):
        map_copy(o).start()

    @pl.loop(1, 16)
    def _(o):
        proj_copy(o).start()

    x[pl.ds(aligned(s * ROWS), ROWS)] = maps[:, pl.ds(aligned(s * 128, 128), 128)]
    wp[:, pl.ds(aligned(s * 16), 16)] = w_proj[...]
    for k in range(3):
        c[k, 0:PAD] = jnp.zeros((PAD, 384), bf16)
        c[k, PAD + PIX : PAD + PIX + PAD] = jnp.zeros((PAD, 384), bf16)

    def build(o, total):
        t = (s + 16 - o) % 16
        at = aligned(t * ROWS)
        raw = x[pl.ds(at, ROWS)]
        v = raw.astype(f32)
        for k, d in enumerate(dilations):
            lo = shifted(v, d, 3, -1).astype(bf16)
            hi = shifted(v, d, 3, 1).astype(bf16)
            c[k, pl.ds(aligned(PAD + at), ROWS)] = jnp.concatenate([lo, raw, hi], axis=1)
        return total + jnp.sum(v.reshape(18, 8, 128), axis=0)

    total = build(0, jnp.zeros((8, 128), f32))

    def build_remote(o, total):
        t = (s + 16 - o) % 16
        links.arrived(x.at[pl.ds(aligned(t * ROWS), ROWS)], x_r.at[o])
        return build(o, total)

    total = lax.fori_loop(1, 16, build_remote, total)
    x_out[...] = x[...]

    pooled = (jnp.sum(total, axis=0, keepdims=True) / PIX).astype(bf16)
    pooled = jnp.broadcast_to(pooled, (16, 128))
    pooled_out[...] = pooled.astype(f32)[0:8]
    pool_part = dot(pooled, w_pool[...])[0:8]
    row = lax.broadcasted_iota(jnp.int32, (8, 256), 0)
    msg[...] = small[...] + jnp.where(row == 0, pool_part, 0.0)
    msgs[pl.ds(s, 1)] = msg[...][None]

    @pl.loop(1, 16)
    def _(o):
        msg_copy(o).start()

    def respond(k):
        @pl.loop(0, PIX // BLOCK)
        def _(i):
            at = aligned(i * BLOCK)
            if k < 3:
                d = dilations[k] * 48
                lhs = jnp.concatenate(
                    [c[k, pl.ds(aligned(PAD + at + (a - 1) * d), BLOCK)] for a in range(3)], axis=1
                )
                p = dot(lhs, w[k])
            else:
                p = dot(c[0, pl.ds(aligned(PAD + at), BLOCK), 128:256], w_point[...])
            part[k, pl.ds(i * (BLOCK // ROWS), BLOCK // ROWS)] = p.reshape(BLOCK // ROWS, ROWS, 256)

        @pl.loop(0, 8)
        def _(j):
            core_out[k, j] = part[k, 2 * j + 1 - core].astype(bf16)

        links.send(core_out.at[k], core_in.at[k], rs_s.at[k, 0], rs_r.at[k, 0], space=sibling)

    def step1(k):
        links.arrived(core_in.at[k], rs_r.at[k, 0])

        @pl.loop(0, 8)
        def _(j):
            acc[k, j] = part[k, 2 * j + core] + core_in[k, j].astype(f32)

        sa[k] = acc[k, x2].astype(bf16)
        links.send(sa.at[k], ra.at[k], rs_s.at[k, 1], rs_r.at[k, 1], space=right)
        sb[k] = acc[k, 4 + x2].astype(bf16)
        links.send(sb.at[k], rb.at[k], rs_s.at[k, 2], rs_r.at[k, 2], space=left)

    def step2(k):
        links.arrived(ra.at[k], rs_r.at[k, 1])
        s2p[k, 0] = (acc[k, xp] + ra[k].astype(f32)).astype(bf16)
        s2p[k, 1] = acc[k, 4 + xp].astype(bf16)
        links.send(s2p.at[k], r2p.at[k], rs_s.at[k, 3], rs_r.at[k, 3], space=right)
        links.arrived(rb.at[k], rs_r.at[k, 2])
        s2m[k, 0] = acc[k, xm].astype(bf16)
        s2m[k, 1] = (acc[k, 4 + xm] + rb[k].astype(f32)).astype(bf16)
        links.send(s2m.at[k], r2m.at[k], rs_s.at[k, 4], rs_r.at[k, 4], space=left)

    def step3(k):
        links.arrived(r2p.at[k], rs_r.at[k, 3])
        links.arrived(r2m.at[k], rs_r.at[k, 4])
        for z in range(2):
            acc[k, z * 4 + cx] = acc[k, z * 4 + cx] + (r2p[k, z].astype(f32) + r2m[k, z].astype(f32))
        sz[k] = acc[k, (1 - cz) * 4 + cx].astype(bf16)
        links.send(sz.at[k], rz.at[k], rs_s.at[k, 5], rs_r.at[k, 5], space=other_z)

    def step4(k):
        links.arrived(rz.at[k], rs_r.at[k, 5])
        return acc[k, cz * 4 + cx] + rz[k].astype(f32)

    respond(0)
    step1(0)
    respond(1)
    step1(1)
    step2(0)
    respond(2)
    step1(2)
    step2(1)
    step3(0)
    respond(3)
    step1(3)
    step2(2)
    step3(1)
    step2(3)

    @pl.loop(1, 16)
    def _(o):
        t = (s + 16 - o) % 16
        links.arrived(msgs.at[t], msg_r.at[o])
        links.arrived(wp.at[:, pl.ds(aligned(t * 16), 16)], wp_r.at[o])

    head_msg = lax.fori_loop(0, 16, lambda i, v: v + msgs[i], jnp.zeros((8, 256), f32))
    pool_pre = head_msg[0:1] + head_msg[5:6]
    pool_out[...] = jnp.broadcast_to(pool_pre, (8, 256))
    pool_act = jnp.broadcast_to(jax.nn.silu(pool_pre).astype(bf16).astype(f32), (ROWS, 256)).astype(bf16)

    step3(2)
    step3(3)

    slopes = []
    acts = []
    for k in range(4):
        pre = step4(k) + head_msg[1 + k : 2 + k]
        sigma = jax.nn.sigmoid(pre)
        slopes.append(sigma * (1.0 + pre * (1.0 - sigma)))
        acts.append((pre * sigma).astype(bf16))
    acts.append(pool_act)
    head = bias_proj[...] + sum(dot(acts[k], wp[k]) for k in range(5))
    sigma = jax.nn.sigmoid(head)
    head_out[...] = (head * sigma).astype(bf16)
    grad_f = cot[...].astype(f32) * (sigma * (1.0 + head * (1.0 - sigma)))
    grad = grad_f.astype(bf16)
    lines = []
    for k in range(4):
        g = (dot_nt(grad, wp[k]) * slopes[k]).astype(bf16)
        grad_pre[k] = g
        lines.append(jnp.sum(g.astype(f32), axis=0, keepdims=True))
    lines.append(jnp.sum(dot_nt(grad, wp[4]), axis=0, keepdims=True))
    lines.append(jnp.sum(grad.astype(f32), axis=0, keepdims=True))
    for i in range(6):
        sums[i : i + 1] = lines[i]
    sums[6:8] = jnp.zeros((2, 256), f32)
    for k in range(5):
        g_proj[k] = lax.dot_general(acts[k], grad, TN, preferred_element_type=f32).astype(bf16)

    @pl.loop(1, 16)
    def _(o):
        map_copy(o).wait_send()
        proj_copy(o).wait_send()
        msg_copy(o).wait_send()

    links.flush()


HALVES = (144, 144, 144, 48)


def backward_kernel(
    x, grad_pre, w, w_point, w_pool, g_proj, sums, pool_pre, pooled,
    d0, d1, d2, d3, maps_out,
    gp, g3, xt, dw0, dw1, dw2, dw3, u1s0, u1s1, u1s2, u1s3, u1r0, u1r1, u1r2, u1r3,
    u2s0, u2s1, u2s2, u2s3, u2r0, u2r1, u2r2, u2r3, es0, es1, es2, es3, zr0, zr1, zr2, zr3,
    zt0, zt1, zt2, zt3, own, gpr, msgs, gx,
    ag_s, ag_r, ar_s, ar_r, gp_s, gp_r, msg_s, msg_r, gx_s, gx_r,
):
    dp = lax.axis_index("dp")
    s = lax.axis_index("space")
    core = s % 2
    cx = (s // 2) % 4
    cz = s // 8
    xp = (cx + 1) % 4
    xm = (cx + 3) % 4
    x2 = (cx + 2) % 4

    def at(z, col, half):
        return (z * 4 + col) * 2 + half

    right = at(cz, xp, core)
    left = at(cz, xm, core)
    other_z = at(1 - cz, cx, core)
    sibling = at(cz, cx, 1 - core)
    y = dp % 4
    hz = dp // 4
    yp = (y + 1) % 4
    ym = (y + 3) % 4
    y2 = (y + 2) % 4
    up = hz * 4 + yp
    down = hz * 4 + ym
    links = Links(dp, s)

    barrier = pltpu.get_barrier_semaphore()

    @pl.loop(1, 16)
    def _(o):
        pl.semaphore_signal(barrier, inc=1, device_id=(dp, (s + o) % 16), device_id_type=MESH)

    pl.semaphore_signal(barrier, inc=1, device_id=(up, s), device_id_type=MESH)
    pl.semaphore_signal(barrier, inc=1, device_id=(down, s), device_id_type=MESH)
    for o in range(1, 4):
        pl.semaphore_signal(barrier, inc=1, device_id=(((hz + o) % 4) * 4 + y, s), device_id_type=MESH)
    pl.semaphore_wait(barrier, 20)

    def block(k, n):
        if k < 3:
            return gp.at[k, pl.ds(aligned(PAD + n * ROWS), ROWS)]
        return g3.at[pl.ds(aligned(n * ROWS), ROWS)]

    def pass_on(k, n, slot, to):
        b = block(k, n)
        links.send(b, b, ag_s.at[k, slot], ag_r.at[k, n], space=to)

    def have(k, n):
        links.arrived(block(k, n), ag_r.at[k, n])

    def own_block(k):
        mine = grad_pre[k]
        if k < 3:
            gp[k, pl.ds(aligned(PAD + s * ROWS), ROWS)] = mine
        else:
            g3[pl.ds(aligned(s * ROWS), ROWS)] = mine
        pass_on(k, s, 0, other_z)
        pass_on(k, s, 1, right)
        pass_on(k, s, 2, left)
        pass_on(k, s, 3, sibling)

    def gather1(k):
        n = at(1 - cz, cx, core)
        have(k, n)
        pass_on(k, n, 4, right)
        pass_on(k, n, 5, left)
        pass_on(k, n, 6, sibling)

    def gather2(k):
        n = at(0, xm, core)
        have(k, n)
        pass_on(k, n, 7, right)
        pass_on(k, n, 8, sibling)
        n = at(1, xp, core)
        have(k, n)
        pass_on(k, n, 9, left)
        pass_on(k, n, 10, sibling)
        n = at(1, xm, core)
        have(k, n)
        pass_on(k, n, 11, sibling)
        n = at(0, xp, core)
        have(k, n)
        pass_on(k, n, 12, sibling)

    def gather3(k):
        for z in range(2):
            n = at(z, x2, core)
            have(k, n)
            pass_on(k, n, 13 + z, sibling)
        for z in range(2):
            for col in (cx, xp, xm, x2):
                have(k, at(z, col, 1 - core))

    for k in range(4):
        own_block(k)

    def proj_copy(o):
        t = (s + o) % 16
        return links.copy(
            g_proj.at[:, pl.ds(aligned(t * 16), 16)], gpr.at[s], gp_s.at[o], gp_r.at[o], dp, t
        )

    def msg_copy(o):
        return links.copy(sums, msgs.at[s], msg_s.at[o], msg_r.at[o], dp, (s + o) % 16)

    @pl.loop(1, 16)
    def _(o):
        msg_copy(o).start()

    for k in range(3):
        gp[k, 0:PAD] = jnp.zeros((PAD, 256), bf16)
        gp[k, PAD + PIX : PAD + PIX + PAD] = jnp.zeros((PAD, 256), bf16)
    msgs[pl.ds(s, 1)] = sums[...][None]
    gpr[pl.ds(s, 1)] = g_proj[:, pl.ds(aligned(s * 16), 16)][None]

    def turn(i):
        st = aligned(i * 384, 128)
        v = x[pl.ds(st, 384)].astype(f32)
        mid = jnp.transpose(v).astype(bf16)
        for k, d in enumerate(dilations):
            xt[k, 0:128, pl.ds(st, 384)] = jnp.transpose(shifted(v, d, 8, -1)).astype(bf16)
            xt[k, 128:256, pl.ds(st, 384)] = mid
            xt[k, 256:384, pl.ds(st, 384)] = jnp.transpose(shifted(v, d, 8, 1)).astype(bf16)

    @pl.loop(0, 2)
    def _(i):
        turn(i)

    gather1(0)
    gather1(1)

    @pl.loop(2, 4)
    def _(i):
        turn(i)

    gather2(0)
    gather1(2)

    @pl.loop(4, 6)
    def _(i):
        turn(i)

    gather2(1)
    gather1(3)

    @pl.loop(1, 16)
    def _(o):
        proj_copy(o).start()

    gather3(0)

    dws = (dw0, dw1, dw2, dw3)
    outs = (d0, d1, d2, d3)
    u1s, u1r = (u1s0, u1s1, u1s2, u1s3), (u1r0, u1r1, u1r2, u1r3)
    u2s, u2r = (u2s0, u2s1, u2s2, u2s3), (u2r0, u2r1, u2r2, u2r3)
    es, zr, zt = (es0, es1, es2, es3), (zr0, zr1, zr2, zr3), (zt0, zt1, zt2, zt3)

    def weight_grad(k):
        d = 48 * dilations[k]
        for a, (lo, hi) in enumerate(
            ((0, -((d - PIX) // 128) * 128), (0, PIX), (d // 128 * 128, PIX))
        ):
            g0 = PAD + lo - (a - 1) * d
            dws[k][384 * a : 384 * (a + 1)] = dot(xt[k, :, lo:hi], gp[k, g0 : g0 + hi - lo])

    def sum1(k):
        h = HALVES[k]
        dw = dws[k]
        u1s[k][0] = dw[pl.ds(aligned(y2 * 2 * h), h)].astype(bf16)
        links.send(u1s[k].at[0], u1r[k].at[0], ar_s.at[k, 0], ar_r.at[k, 0], dp=up)
        u1s[k][1] = dw[pl.ds(aligned(y2 * 2 * h + h), h)].astype(bf16)
        links.send(u1s[k].at[1], u1r[k].at[1], ar_s.at[k, 1], ar_r.at[k, 1], dp=down)

    def sum2(k):
        h = HALVES[k]
        dw = dws[k]
        links.arrived(u1r[k].at[0], ar_r.at[k, 0])
        u2s[k][0, 0] = (dw[pl.ds(aligned(yp * 2 * h), h)] + u1r[k][0].astype(f32)).astype(bf16)
        u2s[k][0, 1] = dw[pl.ds(aligned(yp * 2 * h + h), h)].astype(bf16)
        links.send(u2s[k].at[0], u2r[k].at[0], ar_s.at[k, 2], ar_r.at[k, 2], dp=up)
        links.arrived(u1r[k].at[1], ar_r.at[k, 1])
        u2s[k][1, 0] = dw[pl.ds(aligned(ym * 2 * h), h)].astype(bf16)
        u2s[k][1, 1] = (dw[pl.ds(aligned(ym * 2 * h + h), h)] + u1r[k][1].astype(f32)).astype(bf16)
        links.send(u2s[k].at[1], u2r[k].at[1], ar_s.at[k, 3], ar_r.at[k, 3], dp=down)

    def sum3(k):
        h = HALVES[k]
        dw = dws[k]
        links.arrived(u2r[k].at[0], ar_r.at[k, 2])
        links.arrived(u2r[k].at[1], ar_r.at[k, 3])
        for half in range(2):
            v = dw[pl.ds(aligned(y * 2 * h + half * h), h)] + (
                u2r[k][0, half].astype(f32) + u2r[k][1, half].astype(f32)
            )
            for lane in range(2):
                quarter = v[:, 128 * lane : 128 * (lane + 1)]
                own[k, 2 * half + lane, 0:h] = quarter
                es[k][2 * half + lane] = quarter.astype(bf16)
        for o in range(1, 4):
            q = (hz + o) % 4
            links.send(es[k].at[q], zr[k].at[o - 1], ar_s.at[k, 3 + o], ar_r.at[k, 3 + o], dp=q * 4 + y)

    def sum4(k):
        h = HALVES[k]
        v = own[k, hz, 0:h]
        for o in range(1, 4):
            links.arrived(zr[k].at[o - 1], ar_r.at[k, 3 + o])
            v = v + zr[k][o - 1].astype(f32)
        zt[k][hz] = v.astype(bf16)
        for o in range(1, 4):
            q = (hz + o) % 4
            links.send(zt[k].at[hz], zt[k].at[hz], ar_s.at[k, 6 + o], ar_r.at[k, 6 + o], dp=q * 4 + y)

    def chunk(k, n):
        h = HALVES[k]
        return outs[k].at[pl.ds(aligned(n * 2 * h), 2 * h)]

    def half_chunk(k, n, half):
        h = HALVES[k]
        return outs[k].at[pl.ds(aligned(n * 2 * h + half * h), h)]

    def sum5(k):
        h = HALVES[k]
        for o in range(1, 4):
            links.arrived(zt[k].at[(hz + 4 - o) % 4], ar_r.at[k, 6 + o])
        for half in range(2):
            outs[k][pl.ds(aligned(y * 2 * h + half * h), h)] = jnp.concatenate(
                [zt[k][2 * half], zt[k][2 * half + 1]], axis=1
            )
        mine = chunk(k, y)
        links.send(mine, mine, ar_s.at[k, 10], ar_r.at[k, 10], dp=up)
        links.send(mine, mine, ar_s.at[k, 11], ar_r.at[k, 11], dp=down)

    def sum6(k):
        links.arrived(chunk(k, ym), ar_r.at[k, 10])
        b = half_chunk(k, ym, 0)
        links.send(b, b, ar_s.at[k, 12], ar_r.at[k, 12], dp=up)
        links.arrived(chunk(k, yp), ar_r.at[k, 11])
        b = half_chunk(k, yp, 1)
        links.send(b, b, ar_s.at[k, 13], ar_r.at[k, 13], dp=down)

    def sum7(k):
        links.arrived(half_chunk(k, y2, 0), ar_r.at[k, 12])
        links.arrived(half_chunk(k, y2, 1), ar_r.at[k, 13])

    weight_grad(0)
    sum1(0)
    gather2(2)
    gather3(1)
    weight_grad(1)
    sum1(1)
    sum2(0)
    gather2(3)
    gather3(2)
    weight_grad(2)
    sum1(2)
    sum2(1)
    sum3(0)
    gather3(3)

    dw3[0:128] = dot(xt[0, 128:256, :], g3[...])

    @pl.loop(1, 16)
    def _(o):
        t = (s + 16 - o) % 16
        links.arrived(msgs.at[t], msg_r.at[o])
        links.arrived(gpr.at[t], gp_r.at[o])

    totals = lax.fori_loop(0, 16, lambda i, v: v + msgs[i], jnp.zeros((8, 256), f32))
    pool_grad = (silu_slope(pool_pre[0:1]) * totals[4:5]).astype(bf16)
    pool_row = pool_grad.astype(f32)
    column = jnp.transpose(jnp.broadcast_to(pooled[0:1], (128, 128)))
    dw3[128:256] = jnp.concatenate([column, column], axis=1) * pool_row
    dw3[256:336] = lax.fori_loop(
        0, 16, lambda i, v: v + gpr[i].astype(f32).reshape(80, 256), jnp.zeros((80, 256), f32)
    )
    dw3[336:384] = jnp.zeros((48, 256), f32)
    dw3[336:340] = totals[0:4]
    dw3[340:341] = pool_row
    dw3[341:342] = totals[5:6]
    sum1(3)

    back = dot_nt(jnp.broadcast_to(pool_row, (16, 256)).astype(bf16), w_pool[...])[0:1] / PIX

    def input_grad(i):
        st = i * BLOCK
        result = dot_nt(g3[st : st + BLOCK], w_point[...]) + back
        for k in range(3):
            d = 48 * dilations[k]
            sides = 0.0
            for a in range(3):
                g0 = PAD + st - (a - 1) * d
                g = gp[k, g0 : g0 + BLOCK]
                tap = 384 * a
                ends = jnp.concatenate([w[k, tap : tap + 128], w[k, tap + 256 : tap + 384]], axis=0)
                sides = sides + dot_nt(g, ends)
                result = result + dot_nt(g, w[k, tap + 128 : tap + 256])
            result = result + shifted(sides[:, 0:128], dilations[k], BLOCK // 48, 1)
            result = result + shifted(sides[:, 128:256], dilations[k], BLOCK // 48, -1)
        gx[st : st + BLOCK] = result.astype(bf16)
        for j in range(BLOCK // ROWS):
            n = i * (BLOCK // ROWS) + j

            @pl.when(s != n)
            def _():
                gx_copy(n).start()

    def gx_copy(n):
        return links.copy(
            gx.at[pl.ds(n * ROWS, ROWS)], maps_out.at[:, pl.ds(aligned(s * 128, 128), 128)],
            gx_s.at[n], gx_r.at[s], dp, n,
        )

    input_grad(0)
    sum2(2)
    sum3(1)
    sum4(0)
    sum2(3)
    input_grad(1)
    sum3(2)
    sum4(1)
    sum5(0)
    sum3(3)
    input_grad(2)
    sum4(2)
    sum5(1)
    sum6(0)
    sum4(3)
    input_grad(3)
    sum5(2)
    sum6(1)
    sum7(0)
    sum5(3)
    maps_out[:, pl.ds(aligned(s * 128, 128), 128)] = gx[pl.ds(aligned(s * ROWS), ROWS)]
    sum6(2)
    sum6(3)

    @pl.loop(1, 16)
    def _(o):
        t = (s + o) % 16
        links.arrived(maps_out.at[:, pl.ds(aligned(t * 128, 128), 128)], gx_r.at[t])
        proj_copy(o).wait_send()
        msg_copy(o).wait_send()
        links.copy(
            gx.at[pl.ds(0, ROWS)], gx.at[pl.ds(0, ROWS)], gx_s.at[t], gx_s.at[t], dp, t
        ).wait_send()

    sum7(1)
    sum7(2)
    sum7(3)
    links.flush()


def dma(*shape):
    return pltpu.SemaphoreType.DMA(shape)


def vm(dtype, *shape):
    return pltpu.VMEM(shape, dtype)


def body(feature_maps, w_atrous, w_point, w_pool, bias_branch, w_proj, bias_proj, cotangent):
    s = lax.axis_index("space")
    vmem = pl.BlockSpec(memory_space=pltpu.VMEM)
    maps = feature_maps.reshape(ROWS, 2048)
    w = w_atrous.reshape(3, 1152, 256)
    small = lax.dynamic_update_slice(jnp.zeros((8, 256), f32), bias_branch, (1, s * 16))
    cot = cotangent.reshape(ROWS, 256)
    shape = jax.ShapeDtypeStruct
    head_out, grad_pre, x, g_proj, sums, pool_pre, pooled = pl.pallas_call(
        forward_kernel,
        out_shape=(
            shape((ROWS, 256), bf16), shape((4, ROWS, 256), bf16), shape((PIX, 128), bf16),
            shape((5, 256, 256), bf16), shape((8, 256), f32), shape((8, 256), f32), shape((8, 128), f32),
        ),
        in_specs=[vmem] * 8,
        out_specs=[vmem] * 7,
        scratch_shapes=[
            vm(bf16, PIX, 128), vm(bf16, 3, PIX + 2 * PAD, 384), vm(f32, 4, 16, ROWS, 256),
            vm(bf16, 4, 8, ROWS, 256), vm(bf16, 4, 8, ROWS, 256), vm(f32, 4, 8, ROWS, 256),
            vm(bf16, 4, ROWS, 256), vm(bf16, 4, ROWS, 256), vm(bf16, 4, ROWS, 256), vm(bf16, 4, ROWS, 256),
            vm(bf16, 4, 2, ROWS, 256), vm(bf16, 4, 2, ROWS, 256),
            vm(bf16, 4, 2, ROWS, 256), vm(bf16, 4, 2, ROWS, 256),
            vm(bf16, 4, ROWS, 256), vm(bf16, 4, ROWS, 256), vm(bf16, 5, 256, 256),
            vm(f32, 8, 256), vm(f32, 16, 8, 256),
            dma(16), dma(16), dma(16), dma(16), dma(16), dma(16), dma(4, 6), dma(4, 6),
        ],
        compiler_params=pltpu.CompilerParams(
            collective_id=0, has_side_effects=True, vmem_limit_bytes=VMEM_LIMIT
        ),
        name="aspp_forward",
    )(maps, w, w_point, w_pool, small, w_proj, bias_proj.reshape(1, 256), cot)

    sizes = [8 * h for h in HALVES]
    d0, d1, d2, d3, grad_maps = pl.pallas_call(
        backward_kernel,
        out_shape=tuple(shape((n, 256), bf16) for n in sizes) + (shape((ROWS, 2048), bf16),),
        in_specs=[vmem] * 9,
        out_specs=[vmem] * 5,
        scratch_shapes=[
            vm(bf16, 3, PIX + 2 * PAD, 256), vm(bf16, PIX, 256), vm(bf16, 3, 384, PIX),
            *[vm(f32, n, 256) for n in sizes],
            *[vm(bf16, 2, h, 256) for h in HALVES], *[vm(bf16, 2, h, 256) for h in HALVES],
            *[vm(bf16, 2, 2, h, 256) for h in HALVES], *[vm(bf16, 2, 2, h, 256) for h in HALVES],
            *[vm(bf16, 4, h, 128) for h in HALVES], *[vm(bf16, 3, h, 128) for h in HALVES],
            *[vm(bf16, 4, h, 128) for h in HALVES],
            vm(f32, 4, 4, 144, 128), vm(bf16, 16, 5, 16, 256), vm(f32, 16, 8, 256), vm(bf16, PIX, 128),
            dma(4, 15), dma(4, 16), dma(4, 14), dma(4, 14),
            dma(16), dma(16), dma(16), dma(16), dma(16), dma(16),
        ],
        compiler_params=pltpu.CompilerParams(
            collective_id=1, has_side_effects=True, vmem_limit_bytes=VMEM_LIMIT
        ),
        name="aspp_backward",
    )(x, grad_pre, w, w_point, w_pool, g_proj, sums, pool_pre, pooled)

    grad_atrous = jnp.stack([d.reshape(9, 128, 256) for d in (d0, d1, d2)]).astype(f32)
    rest = d3.astype(f32)
    grad_bias = lax.dynamic_slice(rest[336:341], (0, s * 16), (5, 16))
    return (
        head_out.reshape(1, 3, 48, 256),
        grad_maps.reshape(1, 3, 48, 2048),
        grad_atrous,
        rest[0:128],
        rest[128:256],
        grad_bias,
        rest[256:336].reshape(5, 16, 256),
        rest[341],
    )


def solution(mesh):
    placed = (
        P("dp", "space", None, None),
        P(None, None, "space", None),
        P("space", None),
        P("space", None),
        P(None, "space"),
        P(None, "space", None),
        P(),
        P("dp", "space", None, None),
    )
    return jax.shard_map(
        body,
        mesh=mesh,
        in_specs=placed,
        out_specs=(
            P("dp", "space", None, None),
            P("dp", "space", None, None),
            P(None, None, "space", None),
            P("space", None),
            P("space", None),
            P(None, "space"),
            P(None, "space", None),
            P(),
        ),
        check_vma=False,
    )
```

time: 579 us -> 152 us (0.26); the launches traced: 571 us -> 152 us
  blocking collectives: 179 us -> 0 us
  local copies, waits for them, and re-layouts: 156 us -> 6.17 us
  Pallas kernels: 0 us -> 142 us
  waiting for transfers between devices: 139 us -> 0 us
  matrix products: 43.2 us -> 0 us
  other arithmetic: 22.5 us -> 3.56 us
  starting transfers between devices: 16.1 us -> 0 us
  between operations: 15.4 us -> 0.7 us
    psum x2 -> x0, blocking collectives: 150 us -> none  [the longest x1 88.1 us: body(): lax.psum(grad_bias.astype(jnp.bfloat16), 'dp').astype(jnp.float32)]
    pallas_call x0 -> x2, Pallas kernels: none -> 142 us  [the longest x1 89.7 us: body(): pl.pallas_call(backward_kernel, out_shape=tuple((shape((n, 256), bf16) fo...]
    reduce_scatter x1 -> x0, waiting for transfers between devices: 63.2 us -> none  [body(): lax.psum_scatter(jnp.dot(joined_flat, proj_flat, preferred_element_type=j...]
    psum x1 -> x0, waiting for transfers between devices: 50.1 us -> none  [body(): lax.psum(kernel_grads.astype(jnp.bfloat16), 'dp').astype(jnp.float32)]
    unnamed x173 -> x10, local copies, waits for them, and re-layouts: 46.8 us -> 2.05 us
    dot_general x20 -> x0, matrix products: 43.2 us -> none  [the longest x9 14.5 us: body(): jnp.dot(spread, weights, preferred_element_type=jnp.float32)]
    slice x11 -> x4, local copies, waits for them, and re-layouts: 42.5 us -> 1.93 us  [the longest x1 0.72 us: body(): rest[128:256]]
    unnamed x1 -> x0, blocking collectives: 29.4 us -> none
  transfers between devices with their start and end apart: 8 -> 0, of which waited for: 4 -> 0; matrix products, arithmetic and copies ran while one was open for 21% -> 0% of each run, Pallas kernels for 0% -> 0%
where the time goes in v1:
time: 152 us
  Pallas kernels  142 us (93%)
  local copies, waits for them, and re-layouts  6.17 us (4%)
  other arithmetic  3.56 us (2%)
    pallas_call x1, Pallas kernels, body(): pl.pallas_call(backward_kernel, out_shape=tuple((shape((n, 256), bf16) fo...  89.7 us
    pallas_call x1, Pallas kernels, body(): pl.pallas_call(forward_kernel, out_shape=(shape((ROWS, 256), bf16), shape...  52.1 us
    convert_element_type x1, other arithmetic, body(): jnp.stack([d.reshape(9, 128, 256) for d in (d0, d1, d2)]).astype(f32)  3.56 us

profile of v1, /device:TPU:32, one launch (start us, length us, event | category | flops | bytes accessed | tf_op | source)
XLA Modules:
  0.0 152.2 jit_solution(14284208078755138826)
XLA Ops:
  0.6 1.5 dynamic_update_slice.3.small
  2.2 0.0 copy-start.3
  2.2 0.6 copy-done.3
  2.8 52.1 %aspp_forward.1 = (bf16[144,256]{1,0:T(8,128)(2,1)}, bf16[4,144,256]{2,1,0:T(8,128)(2,1)}, bf16[2304,128]{1,0:T(8,128)(2,1)}, bf16[5,256,256]{2,1,0:T(8,128)(2,1...) custom-call(bf16[144,2048]{1,0:T(8,128)(2,1)} %bitcast.14, bf16[3,1152,256]{2,1,0:T(8,128)(2,1)} %bitcast.11, ...), custom_call_target="tpu_custom_call" | custom-call | tf_op jit(solution)/shard_map/aspp_forward/pallas_call | solution.py:659
  54.9 89.7 %aspp_backward.1 = (bf16[1152,256]{1,0:T(8,128)(2,1)}, bf16[1152,256]{1,0:T(8,128)(2,1)}, bf16[1152,256]{1,0:T(8,128)(2,1)}, bf16[384,256]{1,0:T(8,128)(2,1)}, bf16[144,2048]{1,0:T(8,128)(2,1)}) custom-call(bf16[2304,128]{1,0:T(8,128)(2,1)} %get-tuple-element.21.x, bf16[4,144,256]{2,1,0:T(8,128)(2,1)} %get-tuple-element.22.grad_pre, ...), custom_call_target="tpu_custom_call" | custom-call | tf_op jit(solution)/shard_map/aspp_backward/pallas_call | solution.py:684
  144.5 0.0 copy-start
  144.6 0.0 copy-start.2
  144.6 0.0 copy-start.1
  144.6 3.6 %maximum_convert_fusion = f32[3,9,128,256]{3,2,1,0:T(8,128)} fusion(bf16[1,9,128,256]{3,2,1,0:T(8,128)(2,1)} %bitcast.17, bf16[1,9,128,256]{3,2,1,0:T(8,128)(2,1)} %bitcast.16, bf16[1,9,128,256]{3,2,1,0:T(8,128)(2,1)} %bitcast.15), kind=kLoop, calls=%fused_computation | loop fusion | flops 2654208 | bytes 5308416 | tf_op jit(solution)/shard_map/convert_element_type | solution.py:706
  148.1 0.0 copy-done
  148.1 0.7 fusion
  148.9 0.7 constant_dynamic-slice_fusion
  149.5 0.6 slice.23
  150.2 0.6 slice.24
  150.7 0.0 copy-done.2
  150.7 0.6 copy.19
  151.4 0.0 copy-done.1
  151.4 0.8 copy.20
  (2 shorter events, 0.0 us)
Async XLA Ops:
  2.2 0.6 copy-start.3
  144.5 3.6 %copy-start = (bf16[384,256]{1,0:T(8,128)(2,1)S(1)}, bf16[384,256]{1,0:T(8,128)(2,1)}, u32[]{:S(2)}) copy-start(bf16[384,256]{1,0:T(8,128)(2,1)} %get-tuple-element.31) | copy-start | bytes 589828
  144.6 6.2 %copy-start.2 = (bf16[144,256]{1,0:T(8,128)(2,1)S(1)}, bf16[144,256]{1,0:T(8,128)(2,1)}, u32[]{:S(2)}) copy-start(bf16[144,256]{1,0:T(8,128)(2,1)} %get-tuple-element.20) | copy-start | bytes 221188
  144.6 6.8 %copy-start.1 = (bf16[144,2048]{1,0:T(8,128)(2,1)S(1)}, bf16[144,2048]{1,0:T(8,128)(2,1)}, u32[]{:S(2)}) copy-start(bf16[144,2048]{1,0:T(8,128)(2,1)} %get-tuple-element.27) | copy-start | bytes 1769476

commit v2 on v1

v2 whole, which is shorter than its diff:
```python
import jax
import jax.numpy as jnp
from jax import lax
from jax.experimental import pallas as pl
from jax.experimental.pallas import tpu as pltpu
from jax.sharding import PartitionSpec as P

bf16 = jnp.bfloat16
f32 = jnp.float32
dilations = (6, 12, 18)
MESH = pl.DeviceIdType.MESH
ROWS = 144
PIX = 2304
PAD = 864
NT = (((1,), (1,)), ((), ()))
TN = (((0,), (0,)), ((), ()))
BLOCK = 576
VMEM_LIMIT = 60 * 2**20


def silu_slope(values):
    sigma = jax.nn.sigmoid(values)
    return sigma * (1.0 + values * (1.0 - sigma))


def dot(a, b):
    return jnp.dot(a, b, preferred_element_type=f32)


def dot_nt(a, b):
    return lax.dot_general(a, b, NT, preferred_element_type=f32)


def aligned(value, step=16):
    return value if isinstance(value, int) else pl.multiple_of(value, step)


class Links:
    def __init__(self, dp, space):
        self.dp = dp
        self.space = space
        self.sent = []

    def copy(self, src, dst, ssem, rsem, dp, space):
        return pltpu.make_async_remote_copy(
            src_ref=src, dst_ref=dst, send_sem=ssem, recv_sem=rsem, device_id=(dp, space), device_id_type=MESH
        )

    def send(self, src, dst, ssem, rsem, dp=None, space=None):
        c = self.copy(src, dst, ssem, rsem, self.dp if dp is None else dp, self.space if space is None else space)
        c.start()
        self.sent.append(c)

    def arrived(self, ref, rsem):
        self.copy(ref, ref, rsem, rsem, self.dp, self.space).wait_recv()

    def flush(self):
        for c in self.sent:
            c.wait_send()


def shifted(block, d, rows, sign):
    lanes = block.shape[1]
    v = block.reshape(rows, 48, lanes)
    col = lax.broadcasted_iota(jnp.int32, (rows, 48, lanes), 1)
    if sign < 0:
        v = jnp.where(col >= d, pltpu.roll(v, d, 1), 0.0)
    else:
        v = jnp.where(col < 48 - d, pltpu.roll(v, 48 - d, 1), 0.0)
    return v.reshape(rows * 48, lanes)


HALVES = (144, 144, 144, 48)
SMALL_BLOCK = 288


def aspp_kernel(
    maps, w, w_point, w_pool, bias, w_proj, bias_proj, cot,
    head_out, d0, d1, d2, d3, maps_out,
    x, c, core_out, core_in, acc, sa, sb, ra, rb, s2p, s2m, r2p, r2m, sz, rz, wp, slopes, acts,
    gp, g3, xt, dw0, dw1, dw2, dw3, u1s0, u1s1, u1s2, u1s3, u1r0, u1r1, u1r2, u1r3,
    u2s0, u2s1, u2s2, u2s3, u2r0, u2r1, u2r2, u2r3, es0, es1, es2, es3, zr0, zr1, zr2, zr3,
    zt0, zt1, zt2, zt3, own, gpo, gpi, gps, gpr, note, note_in, note_sum, notes, gx,
    x_s, x_r, wp_s, wp_r, wf_s, wf_r, rs_s, rs_r,
    ag_s, ag_r, ar_s, ar_r, gp_s, gp_r, note_s, note_r, gx_s, gx_r,
):
    dp = lax.axis_index("dp")
    s = lax.axis_index("space")
    core = s % 2
    chip = s // 2
    cx = chip % 4
    cz = chip // 4
    xp = (cx + 1) % 4
    xm = (cx + 3) % 4
    x2 = (cx + 2) % 4

    def at(z, col, half):
        return (z * 4 + col) * 2 + half

    right = at(cz, xp, core)
    left = at(cz, xm, core)
    other_z = at(1 - cz, cx, core)
    sibling = at(cz, cx, 1 - core)
    y = dp % 4
    hz = dp // 4
    yp = (y + 1) % 4
    ym = (y + 3) % 4
    y2 = (y + 2) % 4
    up = hz * 4 + yp
    down = hz * 4 + ym
    links = Links(dp, s)

    barrier = pltpu.get_barrier_semaphore()

    @pl.loop(1, 16)
    def _(o):
        pl.semaphore_signal(barrier, inc=1, device_id=(dp, (s + o) % 16), device_id_type=MESH)

    pl.semaphore_signal(barrier, inc=1, device_id=(up, s), device_id_type=MESH)
    pl.semaphore_signal(barrier, inc=1, device_id=(down, s), device_id_type=MESH)
    for o in range(1, 4):
        pl.semaphore_signal(barrier, inc=1, device_id=(((hz + o) % 4) * 4 + y, s), device_id_type=MESH)
    pl.semaphore_wait(barrier, 20)

    def map_copy(o):
        t = (s + o) % 16
        return links.copy(
            maps.at[:, pl.ds(aligned(t * 128, 128), 128)], x.at[pl.ds(aligned(s * ROWS), ROWS)],
            x_s.at[o], x_r.at[o], dp, t,
        )

    @pl.loop(1, 16)
    def _(o):
        map_copy(o).start()

    x[pl.ds(aligned(s * ROWS), ROWS)] = maps[:, pl.ds(aligned(s * 128, 128), 128)]
    wp[:, pl.ds(aligned(s * 16), 16)] = w_proj[...]
    for k in range(3):
        c[k, 0:PAD] = jnp.zeros((PAD, 384), bf16)
        c[k, PAD + PIX : PAD + PIX + PAD] = jnp.zeros((PAD, 384), bf16)
        gp[k, 0:PAD] = jnp.zeros((PAD, 256), bf16)
        gp[k, PAD + PIX : PAD + PIX + PAD] = jnp.zeros((PAD, 256), bf16)

    def build(o, total):
        t = (s + 16 - o) % 16
        base = aligned(t * ROWS)
        raw = x[pl.ds(base, ROWS)]
        v = raw.astype(f32)
        for k, d in enumerate(dilations):
            lo = shifted(v, d, 3, -1).astype(bf16)
            hi = shifted(v, d, 3, 1).astype(bf16)
            c[k, pl.ds(aligned(PAD + base), ROWS)] = jnp.concatenate([lo, raw, hi], axis=1)
        return total + jnp.sum(v.reshape(18, 8, 128), axis=0)

    total = build(0, jnp.zeros((8, 128), f32))

    def build_remote(o, total):
        t = (s + 16 - o) % 16
        links.arrived(x.at[pl.ds(aligned(t * ROWS), ROWS)], x_r.at[o])
        return build(o, total)

    total = lax.fori_loop(1, 16, build_remote, total)

    def proj_part(t):
        return wp.at[:, pl.ds(aligned(t * 16), 16)]

    def proj_copy(o):
        t = ((chip + o) % 8) * 2 + core
        return links.copy(proj_part(s), proj_part(s), wp_s.at[o], wp_r.at[o], dp, t)

    def proj_forward(o):
        t = ((chip + 8 - o) % 8) * 2 + core
        return links.copy(proj_part(t), proj_part(t), wf_s.at[o], wf_r.at[o], dp, sibling)

    @pl.loop(1, 8)
    def _(o):
        proj_copy(o).start()

    proj_forward(0).start()

    def note_first(n):
        links.send(note.at[n], note_in.at[n], note_s.at[n, 8], note_r.at[n, 8], space=sibling)

    def note_copy(n, o):
        t = ((chip + o) % 8) * 2 + core
        return links.copy(note_sum.at[n], notes.at[n, chip], note_s.at[n, o], note_r.at[n, o], dp, t)

    def note_second(n):
        links.arrived(note_in.at[n], note_r.at[n, 8])
        note_sum[n] = note[n] + note_in[n]
        notes[n, pl.ds(chip, 1)] = note_sum[n][None]

        @pl.loop(1, 8)
        def _(o):
            note_copy(n, o).start()

    def note_total(n):
        @pl.loop(1, 8)
        def _(o):
            links.arrived(notes.at[n, (chip + 8 - o) % 8], note_r.at[n, o])

        return lax.fori_loop(0, 8, lambda i, v: v + notes[n, i], jnp.zeros((8, 256), f32))

    def respond(k, lo, hi):
        @pl.loop(lo, hi)
        def _(i):
            base = aligned(i * BLOCK)
            if k < 3:
                d = dilations[k] * 48
                lhs = jnp.concatenate(
                    [c[k, pl.ds(aligned(PAD + base + (a - 1) * d), BLOCK)] for a in range(3)], axis=1
                )
                p = dot(lhs, w[k])
            else:
                p = dot(c[0, pl.ds(aligned(PAD + base), BLOCK), 128:256], w_point[...])
            p = p.reshape(2, 2, ROWS, 256)
            first = core == 0
            acc[k, pl.ds(i * 2, 2)] = jnp.where(first, p[:, 0], p[:, 1])
            core_out[k, pl.ds(i * 2, 2)] = jnp.where(first, p[:, 1], p[:, 0]).astype(bf16)

        if hi == PIX // BLOCK:
            links.send(core_out.at[k], core_in.at[k], rs_s.at[k, 0], rs_r.at[k, 0], space=sibling)

    def step1(k):
        links.arrived(core_in.at[k], rs_r.at[k, 0])

        @pl.loop(0, 8)
        def _(j):
            acc[k, j] = acc[k, j] + core_in[k, j].astype(f32)

        sa[k] = acc[k, x2].astype(bf16)
        links.send(sa.at[k], ra.at[k], rs_s.at[k, 1], rs_r.at[k, 1], space=right)
        sb[k] = acc[k, 4 + x2].astype(bf16)
        links.send(sb.at[k], rb.at[k], rs_s.at[k, 2], rs_r.at[k, 2], space=left)

    def step2(k):
        links.arrived(ra.at[k], rs_r.at[k, 1])
        s2p[k, 0] = (acc[k, xp] + ra[k].astype(f32)).astype(bf16)
        s2p[k, 1] = acc[k, 4 + xp].astype(bf16)
        links.send(s2p.at[k], r2p.at[k], rs_s.at[k, 3], rs_r.at[k, 3], space=right)
        links.arrived(rb.at[k], rs_r.at[k, 2])
        s2m[k, 0] = acc[k, xm].astype(bf16)
        s2m[k, 1] = (acc[k, 4 + xm] + rb[k].astype(f32)).astype(bf16)
        links.send(s2m.at[k], r2m.at[k], rs_s.at[k, 4], rs_r.at[k, 4], space=left)

    def step3(k):
        links.arrived(r2p.at[k], rs_r.at[k, 3])
        links.arrived(r2m.at[k], rs_r.at[k, 4])
        for z in range(2):
            acc[k, z * 4 + cx] = acc[k, z * 4 + cx] + (r2p[k, z].astype(f32) + r2m[k, z].astype(f32))
        sz[k] = acc[k, (1 - cz) * 4 + cx].astype(bf16)
        links.send(sz.at[k], rz.at[k], rs_s.at[k, 5], rs_r.at[k, 5], space=other_z)

    def step4(k):
        links.arrived(rz.at[k], rs_r.at[k, 5])
        return acc[k, cz * 4 + cx] + rz[k].astype(f32)

    def turn(lo, hi):
        @pl.loop(lo, hi)
        def _(i):
            st = aligned(i * 384, 128)
            v = x[pl.ds(st, 384)].astype(f32)
            mid = jnp.transpose(v).astype(bf16)
            for k, d in enumerate(dilations):
                xt[k, 0:128, pl.ds(st, 384)] = jnp.transpose(shifted(v, d, 8, -1)).astype(bf16)
                xt[k, 128:256, pl.ds(st, 384)] = mid
                xt[k, 256:384, pl.ds(st, 384)] = jnp.transpose(shifted(v, d, 8, 1)).astype(bf16)

    respond(3, 0, 4)

    pooled = (jnp.sum(total, axis=0, keepdims=True) / PIX).astype(bf16)
    pooled = jnp.broadcast_to(pooled, (16, 128))
    pool_part = dot(pooled, w_pool[...])[0:8]
    note[0] = jnp.zeros((8, 256), f32)
    for i in range(16):
        note[0, 1:6, 16 * i : 16 * i + 16] = bias[...]
    row = lax.broadcasted_iota(jnp.int32, (8, 256), 0)
    lane = lax.broadcasted_iota(jnp.int32, (8, 256), 1)
    mine = (lane >= s * 16) & (lane < s * 16 + 16)
    note[0] = jnp.where(row == 0, pool_part, jnp.where(mine, note[0], 0.0))
    note_first(0)

    respond(0, 0, 2)
    step1(3)
    note_second(0)
    respond(0, 2, 4)
    respond(1, 0, 2)
    step1(0)
    step2(3)
    respond(1, 2, 4)

    @pl.loop(1, 8)
    def _(o):
        links.arrived(proj_part(((chip + 8 - o) % 8) * 2 + core), wp_r.at[o])
        proj_forward(o).start()

    respond(2, 0, 2)
    step1(1)
    step2(0)
    respond(2, 2, 4)
    step3(3)
    turn(0, 2)
    step1(2)
    step2(1)
    turn(2, 4)
    step3(0)
    step2(2)

    @pl.loop(0, 8)
    def _(o):
        links.arrived(proj_part(((chip + 8 - o) % 8) * 2 + 1 - core), wf_r.at[o])

    head_note = note_total(0)
    pool_pre = head_note[0:1] + head_note[5:6]
    pool_act = jnp.broadcast_to(jax.nn.silu(pool_pre).astype(bf16).astype(f32), (ROWS, 256)).astype(bf16)

    def absorb(k):
        pre = step4(k) + head_note[1 + k : 2 + k]
        sigma = jax.nn.sigmoid(pre)
        slopes[k] = sigma * (1.0 + pre * (1.0 - sigma))
        act = (pre * sigma).astype(bf16)
        acts[k] = act
        return dot(act, wp[k])

    head = bias_proj[...] + dot(pool_act, wp[4])
    head = head + absorb(3)
    turn(4, 6)
    step3(1)
    head = head + absorb(0)
    head = head + absorb(1)
    step3(2)
    head = head + absorb(2)
    sigma = jax.nn.sigmoid(head)
    grad_f = cot[...].astype(f32) * (sigma * (1.0 + head * (1.0 - sigma)))
    grad = grad_f.astype(bf16)

    def block(k, n):
        if k < 3:
            return gp.at[k, pl.ds(aligned(PAD + n * ROWS), ROWS)]
        return g3.at[pl.ds(aligned(n * ROWS), ROWS)]

    def pass_on(k, n, slot, to):
        b = block(k, n)
        links.send(b, b, ag_s.at[k, slot], ag_r.at[k, n], space=to)

    def have(k, n):
        links.arrived(block(k, n), ag_r.at[k, n])

    def own_block(k):
        g = (dot_nt(grad, wp[k]) * slopes[k]).astype(bf16)
        if k < 3:
            gp[k, pl.ds(aligned(PAD + s * ROWS), ROWS)] = g
        else:
            g3[pl.ds(aligned(s * ROWS), ROWS)] = g
        pass_on(k, s, 0, other_z)
        pass_on(k, s, 1, right)
        pass_on(k, s, 2, left)
        pass_on(k, s, 3, sibling)
        note[1, k : k + 1] = jnp.sum(g.astype(f32), axis=0, keepdims=True)

    def gather1(k):
        n = at(1 - cz, cx, core)
        have(k, n)
        pass_on(k, n, 4, right)
        pass_on(k, n, 5, left)
        pass_on(k, n, 6, sibling)

    def gather2(k):
        n = at(0, xm, core)
        have(k, n)
        pass_on(k, n, 7, right)
        pass_on(k, n, 8, sibling)
        n = at(1, xp, core)
        have(k, n)
        pass_on(k, n, 9, left)
        pass_on(k, n, 10, sibling)
        n = at(1, xm, core)
        have(k, n)
        pass_on(k, n, 11, sibling)
        n = at(0, xp, core)
        have(k, n)
        pass_on(k, n, 12, sibling)

    def gather3(k):
        for z in range(2):
            n = at(z, x2, core)
            have(k, n)
            pass_on(k, n, 13 + z, sibling)
        for z in range(2):
            for col in (cx, xp, xm, x2):
                have(k, at(z, col, 1 - core))

    own_block(0)
    own_block(1)
    own_block(2)
    head_out[...] = (head * sigma).astype(bf16)
    for k in range(5):
        act = acts[k] if k < 4 else pool_act
        g = lax.dot_general(act, grad, TN, preferred_element_type=f32).astype(bf16).reshape(8, 2, 16, 256)
        gpo[0, k] = g[:, 0]
        gpo[1, k] = g[:, 1]
    links.send(gpo.at[1 - core], gpi, gp_s.at[0], gp_r.at[0], space=sibling)
    gather1(0)
    note[1, 4:5] = jnp.sum(dot_nt(grad, wp[4]), axis=0, keepdims=True)
    note[1, 5:6] = jnp.sum(grad.astype(f32), axis=0, keepdims=True)
    note[1, 6:8] = jnp.zeros((2, 256), f32)
    gather1(1)
    gather2(0)
    gather1(2)
    own_block(3)
    note_first(1)
    gather2(1)
    gather3(0)

    dws = (dw0, dw1, dw2, dw3)
    outs = (d0, d1, d2, d3)
    u1s, u1r = (u1s0, u1s1, u1s2, u1s3), (u1r0, u1r1, u1r2, u1r3)
    u2s, u2r = (u2s0, u2s1, u2s2, u2s3), (u2r0, u2r1, u2r2, u2r3)
    es, zr, zt = (es0, es1, es2, es3), (zr0, zr1, zr2, zr3), (zt0, zt1, zt2, zt3)

    def weight_grad(k):
        d = 48 * dilations[k]
        for a, (lo, hi) in enumerate(
            ((0, -((d - PIX) // 128) * 128), (0, PIX), (d // 128 * 128, PIX))
        ):
            g0 = PAD + lo - (a - 1) * d
            dws[k][384 * a : 384 * (a + 1)] = dot(xt[k, :, lo:hi], gp[k, g0 : g0 + hi - lo])

    def sum1(k):
        h = HALVES[k]
        dw = dws[k]
        u1s[k][0] = dw[pl.ds(aligned(y2 * 2 * h), h)].astype(bf16)
        links.send(u1s[k].at[0], u1r[k].at[0], ar_s.at[k, 0], ar_r.at[k, 0], dp=up)
        u1s[k][1] = dw[pl.ds(aligned(y2 * 2 * h + h), h)].astype(bf16)
        links.send(u1s[k].at[1], u1r[k].at[1], ar_s.at[k, 1], ar_r.at[k, 1], dp=down)

    def sum2(k):
        h = HALVES[k]
        dw = dws[k]
        links.arrived(u1r[k].at[0], ar_r.at[k, 0])
        u2s[k][0, 0] = (dw[pl.ds(aligned(yp * 2 * h), h)] + u1r[k][0].astype(f32)).astype(bf16)
        u2s[k][0, 1] = dw[pl.ds(aligned(yp * 2 * h + h), h)].astype(bf16)
        links.send(u2s[k].at[0], u2r[k].at[0], ar_s.at[k, 2], ar_r.at[k, 2], dp=up)
        links.arrived(u1r[k].at[1], ar_r.at[k, 1])
        u2s[k][1, 0] = dw[pl.ds(aligned(ym * 2 * h), h)].astype(bf16)
        u2s[k][1, 1] = (dw[pl.ds(aligned(ym * 2 * h + h), h)] + u1r[k][1].astype(f32)).astype(bf16)
        links.send(u2s[k].at[1], u2r[k].at[1], ar_s.at[k, 3], ar_r.at[k, 3], dp=down)

    def sum3(k):
        h = HALVES[k]
        dw = dws[k]
        links.arrived(u2r[k].at[0], ar_r.at[k, 2])
        links.arrived(u2r[k].at[1], ar_r.at[k, 3])
        for half in range(2):
            v = dw[pl.ds(aligned(y * 2 * h + half * h), h)] + (
                u2r[k][0, half].astype(f32) + u2r[k][1, half].astype(f32)
            )
            for lanes in range(2):
                quarter = v[:, 128 * lanes : 128 * (lanes + 1)]
                own[k, 2 * half + lanes, 0:h] = quarter
                es[k][2 * half + lanes] = quarter.astype(bf16)
        for o in range(1, 4):
            q = (hz + o) % 4
            links.send(es[k].at[q], zr[k].at[o - 1], ar_s.at[k, 3 + o], ar_r.at[k, 3 + o], dp=q * 4 + y)

    def sum4(k):
        h = HALVES[k]
        v = own[k, hz, 0:h]
        for o in range(1, 4):
            links.arrived(zr[k].at[o - 1], ar_r.at[k, 3 + o])
            v = v + zr[k][o - 1].astype(f32)
        zt[k][hz] = v.astype(bf16)
        for o in range(1, 4):
            q = (hz + o) % 4
            links.send(zt[k].at[hz], zt[k].at[hz], ar_s.at[k, 6 + o], ar_r.at[k, 6 + o], dp=q * 4 + y)

    def chunk(k, n):
        h = HALVES[k]
        return outs[k].at[pl.ds(aligned(n * 2 * h), 2 * h)]

    def half_chunk(k, n, half):
        h = HALVES[k]
        return outs[k].at[pl.ds(aligned(n * 2 * h + half * h), h)]

    def sum5(k):
        h = HALVES[k]
        for o in range(1, 4):
            links.arrived(zt[k].at[(hz + 4 - o) % 4], ar_r.at[k, 6 + o])
        for half in range(2):
            outs[k][pl.ds(aligned(y * 2 * h + half * h), h)] = jnp.concatenate(
                [zt[k][2 * half], zt[k][2 * half + 1]], axis=1
            )
        share = chunk(k, y)
        links.send(share, share, ar_s.at[k, 10], ar_r.at[k, 10], dp=up)
        links.send(share, share, ar_s.at[k, 11], ar_r.at[k, 11], dp=down)

    def sum6(k):
        links.arrived(chunk(k, ym), ar_r.at[k, 10])
        b = half_chunk(k, ym, 0)
        links.send(b, b, ar_s.at[k, 12], ar_r.at[k, 12], dp=up)
        links.arrived(chunk(k, yp), ar_r.at[k, 11])
        b = half_chunk(k, yp, 1)
        links.send(b, b, ar_s.at[k, 13], ar_r.at[k, 13], dp=down)

    def sum7(k):
        links.arrived(half_chunk(k, y2, 0), ar_r.at[k, 12])
        links.arrived(half_chunk(k, y2, 1), ar_r.at[k, 13])

    def proj_grad_copy(o):
        j = (chip + o) % 8
        return links.copy(gps.at[:, j], gpr.at[chip], gp_s.at[o], gp_r.at[o], dp, j * 2 + core)

    weight_grad(0)
    sum1(0)
    gather2(2)
    note_second(1)
    links.arrived(gpi, gp_r.at[0])
    gps[...] = (gpo[core].astype(f32) + gpi[...].astype(f32)).astype(bf16)

    @pl.loop(1, 8)
    def _(o):
        proj_grad_copy(o).start()

    gather1(3)
    gather3(1)
    weight_grad(1)
    sum1(1)
    sum2(0)
    gather2(3)
    gather3(2)
    weight_grad(2)
    sum1(2)
    sum2(1)
    sum3(0)
    gather3(3)

    dw3[0:128] = dot(xt[0, 128:256, :], g3[...])
    totals = note_total(1)
    pool_grad = (silu_slope(pool_pre) * totals[4:5]).astype(bf16)
    pool_row = pool_grad.astype(f32)
    column = jnp.transpose(jnp.broadcast_to(pooled[0:1].astype(f32), (128, 128)))
    dw3[128:256] = jnp.concatenate([column, column], axis=1) * pool_row

    @pl.loop(1, 8)
    def _(o):
        links.arrived(gpr.at[(chip + 8 - o) % 8], gp_r.at[o])

    gpr[pl.ds(chip, 1)] = gps[:, pl.ds(chip, 1)].reshape(1, 5, 16, 256)
    dw3[256:336] = lax.fori_loop(
        0, 8, lambda i, v: v + gpr[i].astype(f32).reshape(80, 256), jnp.zeros((80, 256), f32)
    )
    dw3[336:384] = jnp.zeros((48, 256), f32)
    dw3[336:340] = totals[0:4]
    dw3[340:341] = pool_row
    dw3[341:342] = totals[5:6]
    sum1(3)

    back = dot_nt(jnp.broadcast_to(pool_row, (16, 256)).astype(bf16), w_pool[...])[0:1] / PIX

    def input_grad(i):
        size = SMALL_BLOCK
        st = i * size
        result = dot_nt(g3[st : st + size], w_point[...]) + back
        for k in range(3):
            d = 48 * dilations[k]
            sides = 0.0
            for a in range(3):
                g0 = PAD + st - (a - 1) * d
                g = gp[k, g0 : g0 + size]
                tap = 384 * a
                ends = jnp.concatenate([w[k, tap : tap + 128], w[k, tap + 256 : tap + 384]], axis=0)
                sides = sides + dot_nt(g, ends)
                result = result + dot_nt(g, w[k, tap + 128 : tap + 256])
            result = result + shifted(sides[:, 0:128], dilations[k], size // 48, 1)
            result = result + shifted(sides[:, 128:256], dilations[k], size // 48, -1)
        gx[st : st + size] = result.astype(bf16)
        for j in range(size // ROWS):
            n = i * (size // ROWS) + j

            @pl.when(s != n)
            def _():
                gx_copy(n).start()

    def gx_copy(n):
        return links.copy(
            gx.at[pl.ds(n * ROWS, ROWS)], maps_out.at[:, pl.ds(aligned(s * 128, 128), 128)],
            gx_s.at[n], gx_r.at[s], dp, n,
        )

    input_grad(0)
    sum2(2)
    input_grad(1)
    sum3(1)
    sum2(3)
    input_grad(2)
    sum4(0)
    input_grad(3)
    sum3(2)
    sum3(3)
    input_grad(4)
    sum4(1)
    input_grad(5)
    sum5(0)
    sum4(2)
    sum4(3)
    input_grad(6)
    sum5(1)
    sum6(0)
    input_grad(7)
    sum5(2)
    sum5(3)
    sum6(1)
    sum7(0)
    maps_out[:, pl.ds(aligned(s * 128, 128), 128)] = gx[pl.ds(aligned(s * ROWS), ROWS)]
    sum6(2)
    sum6(3)

    @pl.loop(1, 16)
    def _(o):
        t = (s + o) % 16
        links.arrived(maps_out.at[:, pl.ds(aligned(t * 128, 128), 128)], gx_r.at[t])
        map_copy(o).wait_send()
        links.copy(
            gx.at[pl.ds(0, ROWS)], gx.at[pl.ds(0, ROWS)], gx_s.at[t], gx_s.at[t], dp, t
        ).wait_send()

    proj_forward(0).wait_send()

    @pl.loop(1, 8)
    def _(o):
        proj_copy(o).wait_send()
        proj_forward(o).wait_send()
        note_copy(0, o).wait_send()
        note_copy(1, o).wait_send()
        proj_grad_copy(o).wait_send()

    sum7(1)
    sum7(2)
    sum7(3)
    links.flush()


def finish_kernel(head, d0, d1, d2, d3, maps, head_out, maps_out, atrous, point, pool, bias, proj, proj_bias):
    s = lax.axis_index("space")
    head_out[...] = head[...]
    maps_out[...] = maps[...]
    for k, d in enumerate((d0, d1, d2)):
        atrous[k] = d[...].astype(f32)
    point[...] = d3[0:128].astype(f32)
    pool[...] = d3[128:256].astype(f32)
    proj[...] = d3[256:336].astype(f32)
    rows = d3[336:352].astype(f32)
    picked = jnp.zeros((5, 16), f32)
    for i in range(16):
        picked = jnp.where(s == i, rows[0:5, 16 * i : 16 * i + 16], picked)
    bias[...] = picked
    proj_bias[...] = rows[5:6]


def dma(*shape):
    return pltpu.SemaphoreType.DMA(shape)


def vm(dtype, *shape):
    return pltpu.VMEM(shape, dtype)


def body(feature_maps, w_atrous, w_point, w_pool, bias_branch, w_proj, bias_proj, cotangent):
    vmem = pl.BlockSpec(memory_space=pltpu.VMEM)
    shape = jax.ShapeDtypeStruct
    sizes = [8 * h for h in HALVES]
    results = pl.pallas_call(
        aspp_kernel,
        out_shape=(
            shape((ROWS, 256), bf16), *[shape((n, 256), bf16) for n in sizes], shape((ROWS, 2048), bf16),
        ),
        in_specs=[vmem] * 8,
        out_specs=[vmem] * 6,
        scratch_shapes=[
            vm(bf16, PIX, 128), vm(bf16, 3, PIX + 2 * PAD, 384),
            vm(bf16, 4, 8, ROWS, 256), vm(bf16, 4, 8, ROWS, 256), vm(f32, 4, 8, ROWS, 256),
            vm(bf16, 4, ROWS, 256), vm(bf16, 4, ROWS, 256), vm(bf16, 4, ROWS, 256), vm(bf16, 4, ROWS, 256),
            vm(bf16, 4, 2, ROWS, 256), vm(bf16, 4, 2, ROWS, 256),
            vm(bf16, 4, 2, ROWS, 256), vm(bf16, 4, 2, ROWS, 256),
            vm(bf16, 4, ROWS, 256), vm(bf16, 4, ROWS, 256), vm(bf16, 5, 256, 256),
            vm(f32, 4, ROWS, 256), vm(bf16, 4, ROWS, 256),
            vm(bf16, 3, PIX + 2 * PAD, 256), vm(bf16, PIX, 256), vm(bf16, 3, 384, PIX),
            *[vm(f32, n, 256) for n in sizes],
            *[vm(bf16, 2, h, 256) for h in HALVES], *[vm(bf16, 2, h, 256) for h in HALVES],
            *[vm(bf16, 2, 2, h, 256) for h in HALVES], *[vm(bf16, 2, 2, h, 256) for h in HALVES],
            *[vm(bf16, 4, h, 128) for h in HALVES], *[vm(bf16, 3, h, 128) for h in HALVES],
            *[vm(bf16, 4, h, 128) for h in HALVES],
            vm(f32, 4, 4, 144, 128),
            vm(bf16, 2, 5, 8, 16, 256), vm(bf16, 5, 8, 16, 256), vm(bf16, 5, 8, 16, 256),
            vm(bf16, 8, 5, 16, 256),
            vm(f32, 2, 8, 256), vm(f32, 2, 8, 256), vm(f32, 2, 8, 256), vm(f32, 2, 8, 8, 256),
            vm(bf16, PIX, 128),
            dma(16), dma(16), dma(8), dma(8), dma(8), dma(8), dma(4, 6), dma(4, 6),
            dma(4, 15), dma(4, 16), dma(4, 14), dma(4, 14),
            dma(8), dma(8), dma(2, 9), dma(2, 9), dma(16), dma(16),
        ],
        compiler_params=pltpu.CompilerParams(
            collective_id=0, has_side_effects=True, vmem_limit_bytes=VMEM_LIMIT
        ),
        name="aspp",
    )(
        feature_maps.reshape(ROWS, 2048), w_atrous.reshape(3, 1152, 256), w_point, w_pool, bias_branch,
        w_proj, bias_proj.reshape(1, 256), cotangent.reshape(ROWS, 256),
    )
    head_out, grad_maps, atrous, point, pool, bias, proj, proj_bias = pl.pallas_call(
        finish_kernel,
        out_shape=(
            shape((ROWS, 256), bf16), shape((ROWS, 2048), bf16), shape((3, 1152, 256), f32),
            shape((128, 256), f32), shape((128, 256), f32), shape((5, 16), f32), shape((80, 256), f32),
            shape((1, 256), f32),
        ),
        in_specs=[vmem] * 6,
        out_specs=[vmem] * 8,
        compiler_params=pltpu.CompilerParams(vmem_limit_bytes=VMEM_LIMIT),
        name="finish",
    )(*results)
    return (
        head_out.reshape(1, 3, 48, 256),
        grad_maps.reshape(1, 3, 48, 2048),
        atrous.reshape(3, 9, 128, 256),
        point,
        pool,
        bias,
        proj.reshape(5, 16, 256),
        proj_bias.reshape(256),
    )


def solution(mesh):
    placed = (
        P("dp", "space", None, None),
        P(None, None, "space", None),
        P("space", None),
        P("space", None),
        P(None, "space"),
        P(None, "space", None),
        P(),
        P("dp", "space", None, None),
    )
    return jax.shard_map(
        body,
        mesh=mesh,
        in_specs=placed,
        out_specs=(
            P("dp", "space", None, None),
            P("dp", "space", None, None),
            P(None, None, "space", None),
            P("space", None),
            P("space", None),
            P(None, "space"),
            P(None, "space", None),
            P(),
        ),
        check_vma=False,
    )
```

time: 152 us -> 133 us (0.88)
  Pallas kernels: 142 us -> 132 us
  local copies, waits for them, and re-layouts: 6.17 us -> 0 us
  other arithmetic: 3.56 us -> 0 us
    pallas_call x2, Pallas kernels: 142 us -> 132 us  [the longest x1 127 us: body(): pl.pallas_call(aspp_kernel, out_shape=(shape((ROWS, 256), bf16), *[shape(...]
    convert_element_type x1 -> x0, other arithmetic: 3.56 us -> none  [body(): jnp.stack([d.reshape(9, 128, 256) for d in (d0, d1, d2)]).astype(f32)]
    unnamed x10 -> x0, local copies, waits for them, and re-layouts: 2.05 us -> none
    slice x4 -> x0, local copies, waits for them, and re-layouts: 1.93 us -> none  [the longest x1 0.72 us: body(): rest[128:256]]
    dynamic_update_slice x1 -> x0, local copies, waits for them, and re-layouts: 1.52 us -> none  [body(): lax.dynamic_update_slice(jnp.zeros((8, 256), f32), bias_branch, (1, s * 16))]
where the time goes in v2:
time: 133 us
  Pallas kernels  132 us (99%)
    pallas_call x1, Pallas kernels, body(): pl.pallas_call(aspp_kernel, out_shape=(shape((ROWS, 256), bf16), *[shape(...  127 us
    pallas_call x1, Pallas kernels, body(): pl.pallas_call(finish_kernel, out_shape=(shape((ROWS, 256), bf16), shape(...  4.82 us

profile of v2, /device:TPU:32, one launch (start us, length us, event | category | flops | bytes accessed | tf_op | source)
XLA Modules:
  0.0 132.5 jit_solution(7366230448701039805)
XLA Ops:
  0.6 127.0 %aspp.1 = (bf16[144,256]{1,0:T(8,128)(2,1)}, bf16[1152,256]{1,0:T(8,128)(2,1)}, bf16[1152,256]{1,0:T(8,128)(2,1)}, bf16[1152,256]{1,0:T(8,128)(2,1)}, bf16[384,2...) custom-call(bf16[144,2048]{1,0:T(8,128)(2,1)} %bitcast.10, bf16[3,1152,256]{2,1,0:T(8,128)(2,1)} %bitcast.9, ...), custom_call_target="tpu_custom_call" | custom-call | tf_op jit(solution)/shard_map/aspp/pallas_call | solution.py:672
  127.7 4.8 %finish.1 = (bf16[144,256]{1,0:T(8,128)(2,1)}, bf16[144,2048]{1,0:T(8,128)(2,1)}, f32[3,1152,256]{2,1,0:T(8,128)}, f32[128,256]{1,0:T(8,128)}, f32[128,256]{1,0:...) custom-call(bf16[144,256]{1,0:T(8,128)(2,1)} %get-tuple-element.22.head, ...), custom_call_target="tpu_custom_call" | custom-call | tf_op jit(solution)/shard_map/finish/pallas_call | solution.py:710

commit v3 on v2

--- a/solution.py
+++ b/solution.py
@@ -70,20 +70,22 @@
     return v.reshape(rows * 48, lanes)
 
 
-HALVES = (144, 144, 144, 48)
+PIECES = ((0, 0, 2, 96), (0, 2, 3, 48), (1, 0, 2, 96), (1, 2, 3, 48), (2, 0, 2, 96), (2, 2, 3, 48), (3, 0, 1, 48))
+HALVES = tuple(piece[3] for piece in PIECES)
+CUT = 80
 SMALL_BLOCK = 288
 
 
 def aspp_kernel(
-    maps, w, w_point, w_pool, bias, w_proj, bias_proj, cot,
-    head_out, d0, d1, d2, d3, maps_out,
-    x, c, core_out, core_in, acc, sa, sb, ra, rb, s2p, s2m, r2p, r2m, sz, rz, wp, slopes, acts,
-    gp, g3, xt, dw0, dw1, dw2, dw3, u1s0, u1s1, u1s2, u1s3, u1r0, u1r1, u1r2, u1r3,
-    u2s0, u2s1, u2s2, u2s3, u2r0, u2r1, u2r2, u2r3, es0, es1, es2, es3, zr0, zr1, zr2, zr3,
-    zt0, zt1, zt2, zt3, own, gpo, gpi, gps, gpr, note, note_in, note_sum, notes, gx,
-    x_s, x_r, wp_s, wp_r, wf_s, wf_r, rs_s, rs_r,
-    ag_s, ag_r, ar_s, ar_r, gp_s, gp_r, note_s, note_r, gx_s, gx_r,
+    maps_in, w_in, w_point_in, w_pool_in, bias_in, w_proj_in, bias_proj_in, cot_in,
+    head_to, d_to, d3_to, maps_out,
+    maps, w, w_point, w_pool, bias, w_proj, bias_proj, cot, head_out, d, d3,
+    x, c, core_out, core_in, acc, sa, sb, ra, rb, s2p, s2m, r2p, r2m, sz, rz, zs, zin, wp, slopes, acts,
+    gp, g3, xt, dw, dw3, own, gpo, gpi, gps, gpr, note, note_in, note_sum, notes, gx,
+    in_s, out_s, x_s, x_r, wp_s, wp_r, wf_s, wf_r, rs_s, rs_r,
+    ag_s, ag_r, ar_s, ar_r, gp_s, gp_r, note_s, note_r, gx_s, gx_r, *pieces,
 ):
+    u1s, u1r, u2s, u2r, es, zr, zt = [pieces[7 * i : 7 * i + 7] for i in range(7)]
     dp = lax.axis_index("dp")
     s = lax.axis_index("space")
     core = s % 2
@@ -110,6 +112,15 @@
     down = hz * 4 + ym
     links = Links(dp, s)
 
+    loads = [
+        pltpu.make_async_copy(source, target, in_s.at[i])
+        for i, (source, target) in enumerate((
+            (maps_in, maps), (w_proj_in, w_proj), (w_point_in, w_point), (w_pool_in, w_pool), (bias_in, bias),
+            (bias_proj_in, bias_proj), (cot_in, cot), (w_in, w),
+        ))
+    ]
+    for load in loads:
+        load.start()
     barrier = pltpu.get_barrier_semaphore()
 
     @pl.loop(1, 16)
@@ -129,9 +140,14 @@
             x_s.at[o], x_r.at[o], dp, t,
         )
 
+    loads[0].wait()
+
     @pl.loop(1, 16)
     def _(o):
         map_copy(o).start()
+
+    for load in loads[1:7]:
+        load.wait()
 
     x[pl.ds(aligned(s * ROWS), ROWS)] = maps[:, pl.ds(aligned(s * 128, 128), 128)]
     wp[:, pl.ds(aligned(s * 16), 16)] = w_proj[...]
@@ -233,6 +249,46 @@
         sb[k] = acc[k, 4 + x2].astype(bf16)
         links.send(sb.at[k], rb.at[k], rs_s.at[k, 2], rs_r.at[k, 2], space=left)
 
+    def cross1(k):
+        links.arrived(core_in.at[k], rs_r.at[k, 0])
+
+        @pl.loop(0, 8)
+        def _(j):
+            acc[k, j] = acc[k, j] + core_in[k, j].astype(f32)
+
+        @pl.loop(0, 4)
+        def _(j):
+            zs[j] = acc[k, (1 - cz) * 4 + j].astype(bf16)
+
+        links.send(zs, zin, rs_s.at[k, 1], rs_r.at[k, 1], space=other_z)
+
+    def cross2(k):
+        links.arrived(zin, rs_r.at[k, 1])
+
+        @pl.loop(0, 4)
+        def _(j):
+            acc[k, cz * 4 + j] = acc[k, cz * 4 + j] + zin[j].astype(f32)
+
+        sa[k] = acc[k, cz * 4 + x2].astype(bf16)
+        upper, lower = pl.ds(0, CUT), pl.ds(CUT, ROWS - CUT)
+        links.send(sa.at[k, upper], ra.at[k, upper], rs_s.at[k, 2], rs_r.at[k, 2], space=right)
+        links.send(sa.at[k, lower], ra.at[k, lower], rs_s.at[k, 3], rs_r.at[k, 3], space=left)
+
+    def cross3(k):
+        links.arrived(ra.at[k, pl.ds(0, CUT)], rs_r.at[k, 2])
+        s2p[k, 0, 0:CUT] = (acc[k, cz * 4 + xp, 0:CUT] + ra[k, 0:CUT].astype(f32)).astype(bf16)
+        s2p[k, 0, CUT:ROWS] = acc[k, cz * 4 + xp, CUT:ROWS].astype(bf16)
+        links.send(s2p.at[k, 0], r2p.at[k, 0], rs_s.at[k, 4], rs_r.at[k, 4], space=right)
+        links.arrived(ra.at[k, pl.ds(CUT, ROWS - CUT)], rs_r.at[k, 3])
+        s2m[k, 0, 0:CUT] = acc[k, cz * 4 + xm, 0:CUT].astype(bf16)
+        s2m[k, 0, CUT:ROWS] = (acc[k, cz * 4 + xm, CUT:ROWS] + ra[k, CUT:ROWS].astype(f32)).astype(bf16)
+        links.send(s2m.at[k, 0], r2m.at[k, 0], rs_s.at[k, 5], rs_r.at[k, 5], space=left)
+
+    def cross4(k):
+        links.arrived(r2p.at[k, 0], rs_r.at[k, 4])
+        links.arrived(r2m.at[k, 0], rs_r.at[k, 5])
+        return acc[k, cz * 4 + cx] + (r2p[k, 0].astype(f32) + r2m[k, 0].astype(f32))
+
     def step2(k):
         links.arrived(ra.at[k], rs_r.at[k, 1])
         s2p[k, 0] = (acc[k, xp] + ra[k].astype(f32)).astype(bf16)
@@ -280,6 +336,7 @@
     note[0] = jnp.where(row == 0, pool_part, jnp.where(mine, note[0], 0.0))
     note_first(0)
 
+    loads[7].wait()
     respond(0, 0, 2)
     step1(3)
     note_second(0)
@@ -295,14 +352,14 @@
         proj_forward(o).start()
 
     respond(2, 0, 2)
-    step1(1)
+    cross1(1)
     step2(0)
+    step3(3)
     respond(2, 2, 4)
-    step3(3)
     turn(0, 2)
     step1(2)
-    step2(1)
     turn(2, 4)
+    cross2(1)
     step3(0)
     step2(2)
 
@@ -315,7 +372,7 @@
     pool_act = jnp.broadcast_to(jax.nn.silu(pool_pre).astype(bf16).astype(f32), (ROWS, 256)).astype(bf16)
 
     def absorb(k):
-        pre = step4(k) + head_note[1 + k : 2 + k]
+        pre = (cross4(k) if k == 1 else step4(k)) + head_note[1 + k : 2 + k]
         sigma = jax.nn.sigmoid(pre)
         slopes[k] = sigma * (1.0 + pre * (1.0 - sigma))
         act = (pre * sigma).astype(bf16)
@@ -325,10 +382,10 @@
     head = bias_proj[...] + dot(pool_act, wp[4])
     head = head + absorb(3)
     turn(4, 6)
-    step3(1)
+    cross3(1)
+    step3(2)
     head = head + absorb(0)
     head = head + absorb(1)
-    step3(2)
     head = head + absorb(2)
     sigma = jax.nn.sigmoid(head)
     grad_f = cot[...].astype(f32) * (sigma * (1.0 + head * (1.0 - sigma)))
@@ -357,6 +414,10 @@
         pass_on(k, s, 2, left)
         pass_on(k, s, 3, sibling)
         note[1, k : k + 1] = jnp.sum(g.astype(f32), axis=0, keepdims=True)
+
+    def head_store():
+        head_out[...] = (head * sigma).astype(bf16)
+        own_head().start()
 
     def gather1(k):
         n = at(1 - cz, cx, core)
@@ -386,73 +447,73 @@
             n = at(z, x2, core)
             have(k, n)
             pass_on(k, n, 13 + z, sibling)
+
+    def gather4(k):
         for z in range(2):
             for col in (cx, xp, xm, x2):
                 have(k, at(z, col, 1 - core))
 
-    own_block(0)
-    own_block(1)
-    own_block(2)
-    head_out[...] = (head * sigma).astype(bf16)
-    for k in range(5):
-        act = acts[k] if k < 4 else pool_act
-        g = lax.dot_general(act, grad, TN, preferred_element_type=f32).astype(bf16).reshape(8, 2, 16, 256)
-        gpo[0, k] = g[:, 0]
-        gpo[1, k] = g[:, 1]
-    links.send(gpo.at[1 - core], gpi, gp_s.at[0], gp_r.at[0], space=sibling)
-    gather1(0)
-    note[1, 4:5] = jnp.sum(dot_nt(grad, wp[4]), axis=0, keepdims=True)
-    note[1, 5:6] = jnp.sum(grad.astype(f32), axis=0, keepdims=True)
-    note[1, 6:8] = jnp.zeros((2, 256), f32)
-    gather1(1)
-    gather2(0)
-    gather1(2)
-    own_block(3)
-    note_first(1)
-    gather2(1)
-    gather3(0)
-
-    dws = (dw0, dw1, dw2, dw3)
-    outs = (d0, d1, d2, d3)
-    u1s, u1r = (u1s0, u1s1, u1s2, u1s3), (u1r0, u1r1, u1r2, u1r3)
-    u2s, u2r = (u2s0, u2s1, u2s2, u2s3), (u2r0, u2r1, u2r2, u2r3)
-    es, zr, zt = (es0, es1, es2, es3), (zr0, zr1, zr2, zr3), (zt0, zt1, zt2, zt3)
-
-    def weight_grad(k):
+    def proj_grad():
+        for k in range(5):
+            act = acts[k] if k < 4 else pool_act
+            g = lax.dot_general(act, grad, TN, preferred_element_type=f32).astype(bf16)
+            g = g.reshape(8, 2, 16, 256)
+            gpo[0, k] = g[:, 0]
+            gpo[1, k] = g[:, 1]
+        links.send(gpo.at[1 - core], gpi, gp_s.at[0], gp_r.at[0], space=sibling)
+
+    def note_start():
+        note[1, 4:5] = jnp.sum(dot_nt(grad, wp[4]), axis=0, keepdims=True)
+        note[1, 5:6] = jnp.sum(grad.astype(f32), axis=0, keepdims=True)
+        note[1, 6:8] = jnp.zeros((2, 256), f32)
+        note_first(1)
+
+    def weight_grad(p):
+        k, first, last, _ = PIECES[p]
         d = 48 * dilations[k]
         for a, (lo, hi) in enumerate(
             ((0, -((d - PIX) // 128) * 128), (0, PIX), (d // 128 * 128, PIX))
         ):
-            g0 = PAD + lo - (a - 1) * d
-            dws[k][384 * a : 384 * (a + 1)] = dot(xt[k, :, lo:hi], gp[k, g0 : g0 + hi - lo])
+            if first <= a < last:
+                g0 = PAD + lo - (a - 1) * d
+                dw[k, 384 * a : 384 * (a + 1)] = dot(xt[k, :, lo:hi], gp[k, g0 : g0 + hi - lo])
+
+    def summed(p, start, size):
+        k, first, _, _ = PIECES[p]
+        if k == 3:
+            return dw3[pl.ds(aligned(start), size)]
+        return dw[k, pl.ds(aligned(384 * first + start), size)]
+
+    def result(p, start, size):
+        k, first, _, _ = PIECES[p]
+        if k == 3:
+            return d3.at[pl.ds(aligned(start), size)]
+        return d.at[k, pl.ds(aligned(384 * first + start), size)]
 
     def sum1(k):
         h = HALVES[k]
-        dw = dws[k]
-        u1s[k][0] = dw[pl.ds(aligned(y2 * 2 * h), h)].astype(bf16)
+        u1s[k][0] = summed(k, y2 * 2 * h, h).astype(bf16)
         links.send(u1s[k].at[0], u1r[k].at[0], ar_s.at[k, 0], ar_r.at[k, 0], dp=up)
-        u1s[k][1] = dw[pl.ds(aligned(y2 * 2 * h + h), h)].astype(bf16)
+        u1s[k][1] = summed(k, y2 * 2 * h + h, h).astype(bf16)
         links.send(u1s[k].at[1], u1r[k].at[1], ar_s.at[k, 1], ar_r.at[k, 1], dp=down)
 
     def sum2(k):
         h = HALVES[k]
-        dw = dws[k]
         links.arrived(u1r[k].at[0], ar_r.at[k, 0])
-        u2s[k][0, 0] = (dw[pl.ds(aligned(yp * 2 * h), h)] + u1r[k][0].astype(f32)).astype(bf16)
-        u2s[k][0, 1] = dw[pl.ds(aligned(yp * 2 * h + h), h)].astype(bf16)
+        u2s[k][0, 0] = (summed(k, yp * 2 * h, h) + u1r[k][0].astype(f32)).astype(bf16)
+        u2s[k][0, 1] = summed(k, yp * 2 * h + h, h).astype(bf16)
         links.send(u2s[k].at[0], u2r[k].at[0], ar_s.at[k, 2], ar_r.at[k, 2], dp=up)
         links.arrived(u1r[k].at[1], ar_r.at[k, 1])
-        u2s[k][1, 0] = dw[pl.ds(aligned(ym * 2 * h), h)].astype(bf16)
-        u2s[k][1, 1] = (dw[pl.ds(aligned(ym * 2 * h + h), h)] + u1r[k][1].astype(f32)).astype(bf16)
+        u2s[k][1, 0] = summed(k, ym * 2 * h, h).astype(bf16)
+        u2s[k][1, 1] = (summed(k, ym * 2 * h + h, h) + u1r[k][1].astype(f32)).astype(bf16)
         links.send(u2s[k].at[1], u2r[k].at[1], ar_s.at[k, 3], ar_r.at[k, 3], dp=down)
 
     def sum3(k):
         h = HALVES[k]
-        dw = dws[k]
         links.arrived(u2r[k].at[0], ar_r.at[k, 2])
         links.arrived(u2r[k].at[1], ar_r.at[k, 3])
         for half in range(2):
-            v = dw[pl.ds(aligned(y * 2 * h + half * h), h)] + (
+            v = summed(k, y * 2 * h + half * h, h) + (
                 u2r[k][0, half].astype(f32) + u2r[k][1, half].astype(f32)
             )
             for lanes in range(2):
@@ -476,18 +537,18 @@
 
     def chunk(k, n):
         h = HALVES[k]
-        return outs[k].at[pl.ds(aligned(n * 2 * h), 2 * h)]
+        return result(k, n * 2 * h, 2 * h)
 
     def half_chunk(k, n, half):
         h = HALVES[k]
-        return outs[k].at[pl.ds(aligned(n * 2 * h + half * h), h)]
+        return result(k, n * 2 * h + half * h, h)
 
     def sum5(k):
         h = HALVES[k]
         for o in range(1, 4):
             links.arrived(zt[k].at[(hz + 4 - o) % 4], ar_r.at[k, 6 + o])
         for half in range(2):
-            outs[k][pl.ds(aligned(y * 2 * h + half * h), h)] = jnp.concatenate(
+            result(k, y * 2 * h + half * h, h)[...] = jnp.concatenate(
                 [zt[k][2 * half], zt[k][2 * half + 1]], axis=1
             )
         share = chunk(k, y)
@@ -502,65 +563,56 @@
         b = half_chunk(k, yp, 1)
         links.send(b, b, ar_s.at[k, 13], ar_r.at[k, 13], dp=down)
 
+    def store(p):
+        k, first, last, _ = PIECES[p]
+        if k == 3:
+            return pltpu.make_async_copy(d3, d3_to, out_s.at[p])
+        rows = pl.ds(384 * first, 384 * (last - first))
+        return pltpu.make_async_copy(d.at[k, rows], d_to.at[k, rows], out_s.at[p])
+
     def sum7(k):
         links.arrived(half_chunk(k, y2, 0), ar_r.at[k, 12])
         links.arrived(half_chunk(k, y2, 1), ar_r.at[k, 13])
+        store(k).start()
 
     def proj_grad_copy(o):
         j = (chip + o) % 8
         return links.copy(gps.at[:, j], gpr.at[chip], gp_s.at[o], gp_r.at[o], dp, j * 2 + core)
 
-    weight_grad(0)
-    sum1(0)
-    gather2(2)
-    note_second(1)
-    links.arrived(gpi, gp_r.at[0])
-    gps[...] = (gpo[core].astype(f32) + gpi[...].astype(f32)).astype(bf16)
-
-    @pl.loop(1, 8)
-    def _(o):
-        proj_grad_copy(o).start()
-
-    gather1(3)
-    gather3(1)
-    weight_grad(1)
-    sum1(1)
-    sum2(0)
-    gather2(3)
-    gather3(2)
-    weight_grad(2)
-    sum1(2)
-    sum2(1)
-    sum3(0)
-    gather3(3)
-
-    dw3[0:128] = dot(xt[0, 128:256, :], g3[...])
-    totals = note_total(1)
-    pool_grad = (silu_slope(pool_pre) * totals[4:5]).astype(bf16)
-    pool_row = pool_grad.astype(f32)
-    column = jnp.transpose(jnp.broadcast_to(pooled[0:1].astype(f32), (128, 128)))
-    dw3[128:256] = jnp.concatenate([column, column], axis=1) * pool_row
-
-    @pl.loop(1, 8)
-    def _(o):
-        links.arrived(gpr.at[(chip + 8 - o) % 8], gp_r.at[o])
-
-    gpr[pl.ds(chip, 1)] = gps[:, pl.ds(chip, 1)].reshape(1, 5, 16, 256)
-    dw3[256:336] = lax.fori_loop(
-        0, 8, lambda i, v: v + gpr[i].astype(f32).reshape(80, 256), jnp.zeros((80, 256), f32)
-    )
-    dw3[336:384] = jnp.zeros((48, 256), f32)
-    dw3[336:340] = totals[0:4]
-    dw3[340:341] = pool_row
-    dw3[341:342] = totals[5:6]
-    sum1(3)
-
-    back = dot_nt(jnp.broadcast_to(pool_row, (16, 256)).astype(bf16), w_pool[...])[0:1] / PIX
+    def proj_grad_share():
+        links.arrived(gpi, gp_r.at[0])
+        gps[...] = (gpo[core].astype(f32) + gpi[...].astype(f32)).astype(bf16)
+
+        @pl.loop(1, 8)
+        def _(o):
+            proj_grad_copy(o).start()
+
+    def small_grads():
+        dw3[0:128] = dot(xt[0, 128:256, :], g3[...])
+        totals = note_total(1)
+        pool_grad = (silu_slope(pool_pre) * totals[4:5]).astype(bf16)
+        pool_row = pool_grad.astype(f32)
+        column = jnp.transpose(jnp.broadcast_to(pooled[0:1].astype(f32), (128, 128)))
+        dw3[128:256] = jnp.concatenate([column, column], axis=1) * pool_row
+
+        @pl.loop(1, 8)
+        def _(o):
+            links.arrived(gpr.at[(chip + 8 - o) % 8], gp_r.at[o])
+
+        gpr[pl.ds(chip, 1)] = gps[:, pl.ds(chip, 1)].reshape(1, 5, 16, 256)
+        dw3[256:336] = lax.fori_loop(
+            0, 8, lambda i, v: v + gpr[i].astype(f32).reshape(80, 256), jnp.zeros((80, 256), f32)
+        )
+        dw3[336:384] = jnp.zeros((48, 256), f32)
+        dw3[336:340] = totals[0:4]
+        dw3[340:341] = pool_row
+        dw3[341:342] = totals[5:6]
+        return dot_nt(jnp.broadcast_to(pool_row, (16, 256)).astype(bf16), w_pool[...])[0:1] / PIX
 
     def input_grad(i):
         size = SMALL_BLOCK
         st = i * size
-        result = dot_nt(g3[st : st + size], w_point[...]) + back
+        total = dot_nt(g3[st : st + size], w_point[...]) + back
         for k in range(3):
             d = 48 * dilations[k]
             sides = 0.0
@@ -570,10 +622,10 @@
                 tap = 384 * a
                 ends = jnp.concatenate([w[k, tap : tap + 128], w[k, tap + 256 : tap + 384]], axis=0)
                 sides = sides + dot_nt(g, ends)
-                result = result + dot_nt(g, w[k, tap + 128 : tap + 256])
-            result = result + shifted(sides[:, 0:128], dilations[k], size // 48, 1)
-            result = result + shifted(sides[:, 128:256], dilations[k], size // 48, -1)
-        gx[st : st + size] = result.astype(bf16)
+                total = total + dot_nt(g, w[k, tap + 128 : tap + 256])
+            total = total + shifted(sides[:, 0:128], dilations[k], size // 48, 1)
+            total = total + shifted(sides[:, 128:256], dilations[k], size // 48, -1)
+        gx[st : st + size] = total.astype(bf16)
         for j in range(size // ROWS):
             n = i * (size // ROWS) + j
 
@@ -587,38 +639,116 @@
             gx_s.at[n], gx_r.at[s], dp, n,
         )
 
+    def own_maps():
+        return pltpu.make_async_copy(
+            gx.at[pl.ds(aligned(s * ROWS), ROWS)], maps_out.at[:, pl.ds(aligned(s * 128, 128), 128)], out_s.at[7]
+        )
+
+    def own_head():
+        return pltpu.make_async_copy(head_out, head_to, out_s.at[8])
+
+    def collect():
+        own_maps().start()
+
+        @pl.loop(1, 16)
+        def _(o):
+            t = (s + o) % 16
+            links.arrived(maps_out.at[:, pl.ds(aligned(t * 128, 128), 128)], gx_r.at[t])
+
+    own_block(0)
+    own_block(1)
+    gather1(0)
+    gather1(1)
+    own_block(2)
+    gather2(0)
+    proj_grad()
+    head_store()
+    gather2(1)
+    gather1(2)
+    own_block(3)
+    gather3(0)
+    note_start()
+    gather4(0)
+    weight_grad(0)
+    gather3(1)
+    gather1(3)
+    sum1(0)
+    gather2(2)
+    gather4(1)
+    weight_grad(2)
+    sum1(2)
+    weight_grad(3)
+    sum2(0)
+    gather2(3)
+    proj_grad_share()
+    weight_grad(1)
+    gather3(2)
+    sum1(1)
+    sum2(2)
+    sum1(3)
+    gather4(2)
+    note_second(1)
+    weight_grad(4)
+    sum3(0)
+    sum2(1)
+    gather3(3)
+    sum1(4)
+    weight_grad(5)
+    sum3(2)
+    gather4(3)
+    sum2(3)
+    sum3(1)
+    sum1(5)
+    sum2(4)
+    sum4(0)
+    back = small_grads()
+    sum4(2)
+    sum3(3)
+    sum2(5)
+    sum4(1)
     input_grad(0)
-    sum2(2)
+    sum1(6)
+    sum5(0)
     input_grad(1)
-    sum3(1)
-    sum2(3)
+    sum3(5)
+    sum3(4)
+    sum2(6)
+    sum5(2)
+    sum4(3)
+    sum5(1)
+    sum4(5)
+    sum3(6)
+    sum6(0)
+    sum6(2)
+    sum4(4)
+    sum6(1)
+    sum5(3)
     input_grad(2)
-    sum4(0)
     input_grad(3)
-    sum3(2)
-    sum3(3)
+    sum4(6)
+    sum5(5)
     input_grad(4)
-    sum4(1)
+    sum6(3)
+    sum7(0)
+    sum5(4)
+    sum7(1)
     input_grad(5)
-    sum5(0)
-    sum4(2)
-    sum4(3)
+    sum5(6)
     input_grad(6)
-    sum5(1)
-    sum6(0)
+    sum6(5)
     input_grad(7)
-    sum5(2)
-    sum5(3)
-    sum6(1)
-    sum7(0)
-    maps_out[:, pl.ds(aligned(s * 128, 128), 128)] = gx[pl.ds(aligned(s * ROWS), ROWS)]
-    sum6(2)
-    sum6(3)
+    sum6(4)
+    sum6(6)
+    sum7(2)
+    sum7(5)
+    sum7(3)
+    collect()
+    sum7(4)
+    sum7(6)
 
     @pl.loop(1, 16)
     def _(o):
         t = (s + o) % 16
-        links.arrived(maps_out.at[:, pl.ds(aligned(t * 128, 128), 128)], gx_r.at[t])
         map_copy(o).wait_send()
         links.copy(
             gx.at[pl.ds(0, ROWS)], gx.at[pl.ds(0, ROWS)], gx_s.at[t], gx_s.at[t], dp, t
@@ -634,27 +764,58 @@
         note_copy(1, o).wait_send()
         proj_grad_copy(o).wait_send()
 
-    sum7(1)
-    sum7(2)
-    sum7(3)
+    own_maps().wait()
+    own_head().wait()
+    for p in range(7):
+        store(p).wait()
     links.flush()
 
 
-def finish_kernel(head, d0, d1, d2, d3, maps, head_out, maps_out, atrous, point, pool, bias, proj, proj_bias):
+def finish_kernel(
+    head_in, d_in, d3_in, maps_in, head_out, maps_out, atrous, point, pool, bias, proj, proj_bias,
+    d, d3, wide, wide3, maps, head, in_s, out_s,
+):
     s = lax.axis_index("space")
-    head_out[...] = head[...]
-    maps_out[...] = maps[...]
-    for k, d in enumerate((d0, d1, d2)):
-        atrous[k] = d[...].astype(f32)
-    point[...] = d3[0:128].astype(f32)
-    pool[...] = d3[128:256].astype(f32)
-    proj[...] = d3[256:336].astype(f32)
+    loads = [pltpu.make_async_copy(d3_in, d3, in_s.at[6])]
+    loads += [pltpu.make_async_copy(half(d_in, i), half(d, i), in_s.at[i]) for i in range(6)]
+    loads += [pltpu.make_async_copy(maps_in, maps, in_s.at[7]), pltpu.make_async_copy(head_in, head, in_s.at[8])]
+    for copy in loads:
+        copy.start()
+    loads[0].wait()
+    wide3[...] = d3[0:336].astype(f32)
     rows = d3[336:352].astype(f32)
     picked = jnp.zeros((5, 16), f32)
     for i in range(16):
         picked = jnp.where(s == i, rows[0:5, 16 * i : 16 * i + 16], picked)
     bias[...] = picked
     proj_bias[...] = rows[5:6]
+    stores = [
+        pltpu.make_async_copy(wide3.at[pl.ds(0, 128)], point, out_s.at[8]),
+        pltpu.make_async_copy(wide3.at[pl.ds(128, 128)], pool, out_s.at[9]),
+        pltpu.make_async_copy(wide3.at[pl.ds(256, 80)], proj, out_s.at[10]),
+    ]
+    for copy in stores:
+        copy.start()
+    for i in range(6):
+        loads[1 + i].wait()
+        k, first = i // 2, 576 * (i % 2)
+        wide[k, first : first + 576] = d[k, first : first + 576].astype(f32)
+        copy = pltpu.make_async_copy(half(wide, i), half(atrous, i), out_s.at[i])
+        copy.start()
+        stores.append(copy)
+    loads[7].wait()
+    loads[8].wait()
+    through = [
+        pltpu.make_async_copy(maps, maps_out, out_s.at[6]), pltpu.make_async_copy(head, head_out, out_s.at[7]),
+    ]
+    for copy in through:
+        copy.start()
+    for copy in stores + through:
+        copy.wait()
+
+
+def half(array, i):
+    return array.at[i // 2, pl.ds(576 * (i % 2), 576)]
 
 
 def dma(*shape):
@@ -666,38 +827,41 @@
 
 
 def body(feature_maps, w_atrous, w_point, w_pool, bias_branch, w_proj, bias_proj, cotangent):
+    hbm = pl.BlockSpec(memory_space=pl.ANY)
     vmem = pl.BlockSpec(memory_space=pltpu.VMEM)
     shape = jax.ShapeDtypeStruct
-    sizes = [8 * h for h in HALVES]
     results = pl.pallas_call(
         aspp_kernel,
         out_shape=(
-            shape((ROWS, 256), bf16), *[shape((n, 256), bf16) for n in sizes], shape((ROWS, 2048), bf16),
+            shape((ROWS, 256), bf16), shape((3, 1152, 256), bf16), shape((384, 256), bf16),
+            shape((ROWS, 2048), bf16),
         ),
-        in_specs=[vmem] * 8,
-        out_specs=[vmem] * 6,
+        in_specs=[hbm] * 8,
+        out_specs=[hbm] * 4,
         scratch_shapes=[
+            vm(bf16, ROWS, 2048), vm(bf16, 3, 1152, 256), vm(bf16, 128, 256), vm(bf16, 128, 256), vm(f32, 5, 16),
+            vm(bf16, 5, 16, 256), vm(f32, 1, 256), vm(bf16, ROWS, 256),
+            vm(bf16, ROWS, 256), vm(bf16, 3, 1152, 256), vm(bf16, 384, 256),
             vm(bf16, PIX, 128), vm(bf16, 3, PIX + 2 * PAD, 384),
             vm(bf16, 4, 8, ROWS, 256), vm(bf16, 4, 8, ROWS, 256), vm(f32, 4, 8, ROWS, 256),
             vm(bf16, 4, ROWS, 256), vm(bf16, 4, ROWS, 256), vm(bf16, 4, ROWS, 256), vm(bf16, 4, ROWS, 256),
             vm(bf16, 4, 2, ROWS, 256), vm(bf16, 4, 2, ROWS, 256),
             vm(bf16, 4, 2, ROWS, 256), vm(bf16, 4, 2, ROWS, 256),
-            vm(bf16, 4, ROWS, 256), vm(bf16, 4, ROWS, 256), vm(bf16, 5, 256, 256),
-            vm(f32, 4, ROWS, 256), vm(bf16, 4, ROWS, 256),
+            vm(bf16, 4, ROWS, 256), vm(bf16, 4, ROWS, 256), vm(bf16, 4, ROWS, 256), vm(bf16, 4, ROWS, 256),
+            vm(bf16, 5, 256, 256), vm(f32, 4, ROWS, 256), vm(bf16, 4, ROWS, 256),
             vm(bf16, 3, PIX + 2 * PAD, 256), vm(bf16, PIX, 256), vm(bf16, 3, 384, PIX),
-            *[vm(f32, n, 256) for n in sizes],
+            vm(f32, 3, 1152, 256), vm(f32, 384, 256), vm(f32, 7, 4, 96, 128),
+            vm(bf16, 2, 5, 8, 16, 256), vm(bf16, 5, 8, 16, 256), vm(bf16, 5, 8, 16, 256),
+            vm(bf16, 8, 5, 16, 256),
+            vm(f32, 2, 8, 256), vm(f32, 2, 8, 256), vm(f32, 2, 8, 256), vm(f32, 2, 8, 8, 256),
+            vm(bf16, PIX, 128),
+            dma(8), dma(9), dma(16), dma(16), dma(8), dma(8), dma(8), dma(8), dma(4, 6), dma(4, 6),
+            dma(4, 15), dma(4, 16), dma(7, 14), dma(7, 14),
+            dma(8), dma(8), dma(2, 9), dma(2, 9), dma(16), dma(16),
             *[vm(bf16, 2, h, 256) for h in HALVES], *[vm(bf16, 2, h, 256) for h in HALVES],
             *[vm(bf16, 2, 2, h, 256) for h in HALVES], *[vm(bf16, 2, 2, h, 256) for h in HALVES],
             *[vm(bf16, 4, h, 128) for h in HALVES], *[vm(bf16, 3, h, 128) for h in HALVES],
             *[vm(bf16, 4, h, 128) for h in HALVES],
-            vm(f32, 4, 4, 144, 128),
-            vm(bf16, 2, 5, 8, 16, 256), vm(bf16, 5, 8, 16, 256), vm(bf16, 5, 8, 16, 256),
-            vm(bf16, 8, 5, 16, 256),
-            vm(f32, 2, 8, 256), vm(f32, 2, 8, 256), vm(f32, 2, 8, 256), vm(f32, 2, 8, 8, 256),
-            vm(bf16, PIX, 128),
-            dma(16), dma(16), dma(8), dma(8), dma(8), dma(8), dma(4, 6), dma(4, 6),
-            dma(4, 15), dma(4, 16), dma(4, 14), dma(4, 14),
-            dma(8), dma(8), dma(2, 9), dma(2, 9), dma(16), dma(16),
         ],
         compiler_params=pltpu.CompilerParams(
             collective_id=0, has_side_effects=True, vmem_limit_bytes=VMEM_LIMIT
@@ -714,8 +878,12 @@
             shape((128, 256), f32), shape((128, 256), f32), shape((5, 16), f32), shape((80, 256), f32),
             shape((1, 256), f32),
         ),
-        in_specs=[vmem] * 6,
-        out_specs=[vmem] * 8,
+        in_specs=[hbm] * 4,
+        out_specs=[hbm] * 5 + [vmem, hbm, vmem],
+        scratch_shapes=[
+            vm(bf16, 3, 1152, 256), vm(bf16, 384, 256), vm(f32, 3, 1152, 256), vm(f32, 336, 256),
+            vm(bf16, ROWS, 2048), vm(bf16, ROWS, 256), dma(9), dma(11),
+        ],
         compiler_params=pltpu.CompilerParams(vmem_limit_bytes=VMEM_LIMIT),
         name="finish",
     )(*results)

time: 133 us -> 123 us (0.925)
  Pallas kernels: 132 us -> 122 us
    pallas_call x1, Pallas kernels: 127 us -> 117 us  [body(): pl.pallas_call(aspp_kernel, out_shape=(shape((ROWS, 256), bf16), shape((3...]
where the time goes in v3:
time: 123 us
  Pallas kernels  122 us (99%)
    pallas_call x1, Pallas kernels, body(): pl.pallas_call(aspp_kernel, out_shape=(shape((ROWS, 256), bf16), shape((3...  117 us
    pallas_call x1, Pallas kernels, body(): pl.pallas_call(finish_kernel, out_shape=(shape((ROWS, 256), bf16), shape(...  4.82 us

profile of v3, /device:TPU:32, one launch (start us, length us, event | category | flops | bytes accessed | tf_op | source)
XLA Modules:
  0.0 122.9 jit_solution(4380996889954053154)
XLA Ops:
  0.6 117.3 %aspp.1 = (bf16[144,256]{1,0:T(8,128)(2,1)}, bf16[3,1152,256]{2,1,0:T(8,128)(2,1)}, bf16[384,256]{1,0:T(8,128)(2,1)}, bf16[144,2048]{1,0:T(8,128)(2,1)}) custom-call(bf16[144,2048]{1,0:T(8,128)(2,1)} %bitcast.10, bf16[3,1152,256]{2,1,0:T(8,128)(2,1)} %bitcast.9, bf16[128,256]{1,0:T(8,128)(2,1)} %w_point_in.1, bf16[128,256]{1,0:T(8,128)(2,1)} %w_pool_in.1, ...), custom_call_target="tpu_custom_call" | custom-call | tf_op jit(solution)/shard_map/aspp/pallas_call | solution.py:833
  117.9 4.8 %finish.1 = (bf16[144,256]{1,0:T(8,128)(2,1)}, bf16[144,2048]{1,0:T(8,128)(2,1)}, f32[3,1152,256]{2,1,0:T(8,128)}, f32[128,256]{1,0:T(8,128)}, f32[128,256]{1,0:...) custom-call(bf16[144,256]{1,0:T(8,128)(2,1)} %get-tuple-element.20.head_in, ...), custom_call_target="tpu_custom_call" | custom-call | tf_op jit(solution)/shard_map/finish/pallas_call | solution.py:874

commit v4 on v3

--- a/solution.py
+++ b/solution.py
@@ -655,95 +655,95 @@
             t = (s + o) % 16
             links.arrived(maps_out.at[:, pl.ds(aligned(t * 128, 128), 128)], gx_r.at[t])
 
+    own_block(1)
+    own_block(2)
     own_block(0)
-    own_block(1)
-    gather1(0)
-    gather1(1)
-    own_block(2)
-    gather2(0)
     proj_grad()
     head_store()
+    gather1(1)
+    gather1(2)
+    gather1(0)
     gather2(1)
-    gather1(2)
     own_block(3)
-    gather3(0)
+    gather2(2)
     note_start()
-    gather4(0)
-    weight_grad(0)
+    gather2(0)
     gather3(1)
-    gather1(3)
-    sum1(0)
-    gather2(2)
     gather4(1)
     weight_grad(2)
     sum1(2)
+    gather3(2)
+    gather1(3)
+    proj_grad_share()
     weight_grad(3)
+    gather4(2)
+    sum1(3)
+    weight_grad(5)
+    sum1(5)
+    gather3(0)
+    sum2(2)
+    weight_grad(4)
+    sum1(4)
+    sum2(3)
+    gather4(0)
+    sum2(5)
+    gather2(3)
+    weight_grad(1)
+    sum1(1)
+    note_second(1)
+    sum3(2)
+    sum2(4)
+    weight_grad(0)
+    sum1(0)
+    sum3(5)
+    sum3(3)
+    sum2(1)
+    sum4(2)
+    gather3(3)
+    sum3(4)
     sum2(0)
-    gather2(3)
-    proj_grad_share()
-    weight_grad(1)
-    gather3(2)
-    sum1(1)
-    sum2(2)
-    sum1(3)
-    gather4(2)
-    note_second(1)
-    weight_grad(4)
+    gather4(3)
+    back = small_grads()
+    sum3(1)
+    sum4(3)
+    sum1(6)
+    input_grad(0)
+    sum5(2)
     sum3(0)
-    sum2(1)
-    gather3(3)
-    sum1(4)
-    weight_grad(5)
-    sum3(2)
-    gather4(3)
-    sum2(3)
-    sum3(1)
-    sum1(5)
-    sum2(4)
+    sum2(6)
+    sum4(1)
+    sum4(4)
+    sum6(2)
+    sum5(3)
+    sum3(6)
+    sum4(5)
     sum4(0)
-    back = small_grads()
-    sum4(2)
-    sum3(3)
-    sum2(5)
-    sum4(1)
-    input_grad(0)
-    sum1(6)
+    input_grad(1)
+    sum5(1)
+    sum5(4)
+    sum7(2)
+    sum6(3)
+    sum4(6)
+    input_grad(2)
+    sum5(5)
+    input_grad(3)
+    sum6(1)
     sum5(0)
-    input_grad(1)
-    sum3(5)
-    sum3(4)
-    sum2(6)
-    sum5(2)
-    sum4(3)
-    sum5(1)
-    sum4(5)
-    sum3(6)
-    sum6(0)
-    sum6(2)
-    sum4(4)
-    sum6(1)
-    sum5(3)
-    input_grad(2)
-    input_grad(3)
-    sum4(6)
-    sum5(5)
     input_grad(4)
-    sum6(3)
-    sum7(0)
-    sum5(4)
-    sum7(1)
     input_grad(5)
     sum5(6)
+    sum6(4)
+    sum6(5)
     input_grad(6)
-    sum6(5)
     input_grad(7)
-    sum6(4)
+    sum6(0)
     sum6(6)
-    sum7(2)
     sum7(5)
+    sum7(4)
+    collect()
+    sum7(1)
+    sum7(0)
     sum7(3)
-    collect()
-    sum7(4)
     sum7(6)
 
     @pl.loop(1, 16)

time: 123 us -> 121 us (0.984)
  Pallas kernels: 122 us -> 119 us
    pallas_call x1, Pallas kernels: 117 us -> 114 us  [body(): pl.pallas_call(aspp_kernel, out_shape=(shape((ROWS, 256), bf16), shape((3...]
where the time goes in v4:
time: 121 us; the launch traced here: 120 us
  Pallas kernels  119 us (98%)
    pallas_call x1, Pallas kernels, body(): pl.pallas_call(aspp_kernel, out_shape=(shape((ROWS, 256), bf16), shape((3...  114 us
    pallas_call x1, Pallas kernels, body(): pl.pallas_call(finish_kernel, out_shape=(shape((ROWS, 256), bf16), shape(...  4.82 us

profile of v4, /device:TPU:32, one launch (start us, length us, event | category | flops | bytes accessed | tf_op | source)
XLA Modules:
  0.0 120.0 jit_solution(8423738035963485060)
XLA Ops:
  0.6 114.4 %aspp.1 = (bf16[144,256]{1,0:T(8,128)(2,1)}, bf16[3,1152,256]{2,1,0:T(8,128)(2,1)}, bf16[384,256]{1,0:T(8,128)(2,1)}, bf16[144,2048]{1,0:T(8,128)(2,1)}) custom-call(bf16[144,2048]{1,0:T(8,128)(2,1)} %bitcast.10, bf16[3,1152,256]{2,1,0:T(8,128)(2,1)} %bitcast.9, bf16[128,256]{1,0:T(8,128)(2,1)} %w_point_in.1, bf16[128,256]{1,0:T(8,128)(2,1)} %w_pool_in.1, ...), custom_call_target="tpu_custom_call" | custom-call | tf_op jit(solution)/shard_map/aspp/pallas_call | solution.py:833
  115.0 4.8 %finish.1 = (bf16[144,256]{1,0:T(8,128)(2,1)}, bf16[144,2048]{1,0:T(8,128)(2,1)}, f32[3,1152,256]{2,1,0:T(8,128)}, f32[128,256]{1,0:T(8,128)}, f32[128,256]{1,0:...) custom-call(bf16[144,256]{1,0:T(8,128)(2,1)} %get-tuple-element.20.head_in, ...), custom_call_target="tpu_custom_call" | custom-call | tf_op jit(solution)/shard_map/finish/pallas_call | solution.py:874

commit v5 on v3

--- a/solution.py
+++ b/solution.py
@@ -655,96 +655,96 @@
             t = (s + o) % 16
             links.arrived(maps_out.at[:, pl.ds(aligned(t * 128, 128), 128)], gx_r.at[t])
 
+    own_block(2)
     own_block(0)
     own_block(1)
-    gather1(0)
-    gather1(1)
-    own_block(2)
-    gather2(0)
+    gather1(2)
     proj_grad()
     head_store()
+    gather1(0)
+    own_block(3)
+    gather2(2)
+    note_start()
+    gather1(1)
+    gather2(0)
+    gather3(2)
+    gather1(3)
+    note_second(1)
+    gather4(2)
+    weight_grad(5)
     gather2(1)
-    gather1(2)
-    own_block(3)
+    sum1(5)
     gather3(0)
-    note_start()
+    weight_grad(4)
+    sum1(4)
     gather4(0)
     weight_grad(0)
+    sum1(0)
+    gather2(3)
+    sum2(5)
     gather3(1)
-    gather1(3)
-    sum1(0)
-    gather2(2)
+    proj_grad_share()
+    sum2(4)
+    weight_grad(1)
+    sum1(1)
     gather4(1)
     weight_grad(2)
+    sum2(0)
+    sum3(5)
+    gather3(3)
+    weight_grad(3)
+    sum1(3)
     sum1(2)
-    weight_grad(3)
-    sum2(0)
-    gather2(3)
-    proj_grad_share()
-    weight_grad(1)
-    gather3(2)
-    sum1(1)
+    sum3(4)
+    gather4(3)
+    sum2(1)
+    back = small_grads()
+    sum1(6)
+    sum4(5)
+    sum2(3)
+    sum3(0)
     sum2(2)
-    sum1(3)
-    gather4(2)
-    note_second(1)
-    weight_grad(4)
-    sum3(0)
-    sum2(1)
-    gather3(3)
-    sum1(4)
-    weight_grad(5)
+    sum4(4)
+    sum5(5)
+    sum3(1)
+    sum3(3)
+    sum2(6)
     sum3(2)
-    gather4(3)
-    sum2(3)
-    sum3(1)
-    sum1(5)
-    sum2(4)
     sum4(0)
-    back = small_grads()
+    input_grad(0)
+    sum5(4)
+    sum3(6)
+    sum4(3)
     sum4(2)
-    sum3(3)
-    sum2(5)
+    sum6(4)
+    sum5(0)
     sum4(1)
-    input_grad(0)
-    sum1(6)
-    sum5(0)
+    sum6(5)
+    sum4(6)
     input_grad(1)
-    sum3(5)
-    sum3(4)
-    sum2(6)
-    sum5(2)
-    sum4(3)
-    sum5(1)
-    sum4(5)
-    sum3(6)
-    sum6(0)
-    sum6(2)
-    sum4(4)
-    sum6(1)
     sum5(3)
     input_grad(2)
+    sum5(2)
     input_grad(3)
-    sum4(6)
-    sum5(5)
     input_grad(4)
+    sum5(6)
+    sum5(1)
+    input_grad(5)
+    sum7(4)
+    sum6(0)
     sum6(3)
-    sum7(0)
-    sum5(4)
-    sum7(1)
-    input_grad(5)
-    sum5(6)
     input_grad(6)
-    sum6(5)
+    sum6(2)
     input_grad(7)
-    sum6(4)
     sum6(6)
-    sum7(2)
-    sum7(5)
+    sum6(1)
     sum7(3)
     collect()
-    sum7(4)
+    sum7(5)
+    sum7(0)
     sum7(6)
+    sum7(2)
+    sum7(1)
 
     @pl.loop(1, 16)
     def _(o):

time: 123 us -> 123 us (level); the launches traced: 123 us -> 122 us
    pallas_call x1, Pallas kernels: 117 us -> 116 us  [body(): pl.pallas_call(aspp_kernel, out_shape=(shape((ROWS, 256), bf16), shape((3...]
where the time goes in v5:
time: 123 us; the launch traced here: 122 us
  Pallas kernels  121 us (98%)
    pallas_call x1, Pallas kernels, body(): pl.pallas_call(aspp_kernel, out_shape=(shape((ROWS, 256), bf16), shape((3...  116 us
    pallas_call x1, Pallas kernels, body(): pl.pallas_call(finish_kernel, out_shape=(shape((ROWS, 256), bf16), shape(...  4.82 us

profile of v5, /device:TPU:32, one launch (start us, length us, event | category | flops | bytes accessed | tf_op | source)
XLA Modules:
  0.0 121.6 jit_solution(10587967446801203357)
XLA Ops:
  0.6 116.0 %aspp.1 = (bf16[144,256]{1,0:T(8,128)(2,1)}, bf16[3,1152,256]{2,1,0:T(8,128)(2,1)}, bf16[384,256]{1,0:T(8,128)(2,1)}, bf16[144,2048]{1,0:T(8,128)(2,1)}) custom-call(bf16[144,2048]{1,0:T(8,128)(2,1)} %bitcast.10, bf16[3,1152,256]{2,1,0:T(8,128)(2,1)} %bitcast.9, bf16[128,256]{1,0:T(8,128)(2,1)} %w_point_in.1, bf16[128,256]{1,0:T(8,128)(2,1)} %w_pool_in.1, ...), custom_call_target="tpu_custom_call" | custom-call | tf_op jit(solution)/shard_map/aspp/pallas_call | solution.py:833
  116.6 4.8 %finish.1 = (bf16[144,256]{1,0:T(8,128)(2,1)}, bf16[144,2048]{1,0:T(8,128)(2,1)}, f32[3,1152,256]{2,1,0:T(8,128)}, f32[128,256]{1,0:T(8,128)}, f32[128,256]{1,0:...) custom-call(bf16[144,256]{1,0:T(8,128)(2,1)} %get-tuple-element.20.head_in, ...), custom_call_target="tpu_custom_call" | custom-call | tf_op jit(solution)/shard_map/finish/pallas_call | solution.py:874
